TPU v7x, 256 devices: a whole 4x4x8 slice. The times are simulated.
256 devices in a mesh: segment: 32 (over z_hi, x, core), tensor: 8 (over y, z_lo).
Axes of the slice: x: 4, y: 4, z: 8 (z_hi: 4, z_lo: 2; z = z_hi * 2 + z_lo), core: 2. Of those that a mesh axis runs over, the one named last changes fastest.
Arguments:
- queries: bfloat16 [32, 256, 8192], P('segment', None, 'tensor'), may hold values from -1280 to 1280
- grad_attended: bfloat16 [32, 256, 8192], P('segment', None, 'tensor'), may hold values from -6 to 6
- vision: bfloat16 [512, 8192], P('segment', 'tensor'), may hold values from -6 to 6
- key_weight: bfloat16 [32, 4096, 1024], P('segment', None, 'tensor'), may hold values from -1 to 1
- value_weight: bfloat16 [32, 4096, 1024], P('segment', None, 'tensor'), may hold values from -0.0625 to 0.0625
- tile_limit: int32 [512], replicated, may hold values from 1 to 4
Outputs:
- attended: bfloat16 [32, 256, 8192], P('segment', None, 'tensor')
- grad_queries: bfloat16 [32, 256, 8192], P('segment', None, 'tensor')
- grad_vision: float32 [512, 8192], P('segment', 'tensor')
Inputs may be any that keep to these rules, and one draw needn't show every extreme that they name: Text token t sees image tokens 0 to tile_limit[t] * 128 - 1.
All inputs are finite; a program needn't handle non-finite values.
Results may differ from a plain program's by a relative error of at most 0.035.
The roundings to bfloat16 on the way count: a program that leaves them out, or rounds other values in their place, can miss the bound.
Values may be sent and summed in bfloat16 or wider, within the bound.
A program may use at most 128 MiB of HBM per device.

v0:
```python
import jax
import jax.numpy as jnp
from jax import lax
from jax.sharding import PartitionSpec as P

HD = 128
TILES = 4


epsilon = 1e-05


def from_partner(value, axis, stride):
    mask = 2**stride
    pairs = [(source, source ^ mask) for source in range(lax.axis_size(axis))]
    return lax.ppermute(value, axis, pairs)


def normalize(pre):
    return pre * lax.rsqrt(jnp.mean(pre * pre, axis=-1, keepdims=True) + epsilon)


def attend(query, grad_out, keys, values, limit, tile_tokens):
    score_scale = HD ** (-0.5)
    scores = (
        jnp.einsum("rkgd,nkd->rkgn", query, keys, preferred_element_type=jnp.float32) * score_scale
    )
    positions = jnp.arange(keys.shape[0], dtype=jnp.int32)
    allowed = (positions[None, :] < (limit * tile_tokens)[:, None])[:, None, None, :]
    scores = jnp.where(allowed, scores, -1e30)
    row_max = jnp.max(scores, axis=-1, keepdims=True)
    shifted = jnp.exp(scores - row_max)
    probability = shifted / jnp.sum(shifted, axis=-1, keepdims=True)
    prob_low = probability.astype(jnp.bfloat16)
    output = jnp.einsum(
        "rkgn,nkd->rkgd", prob_low, values, preferred_element_type=jnp.float32
    ).astype(jnp.bfloat16)
    grad_prob = jnp.einsum("rkgd,nkd->rkgn", grad_out, values, preferred_element_type=jnp.float32)
    delta = jnp.sum(
        grad_out.astype(jnp.float32) * output.astype(jnp.float32), axis=-1, keepdims=True
    )
    grad_score = (probability * (grad_prob - delta)).astype(jnp.bfloat16)
    grad_query = (
        jnp.einsum("rkgn,nkd->rkgd", grad_score, keys, preferred_element_type=jnp.float32)
        * score_scale
    ).astype(jnp.bfloat16)
    grad_keys = (
        jnp.einsum("rkgn,rkgd->nkd", grad_score, query, preferred_element_type=jnp.float32)
        * score_scale
    )
    grad_values = jnp.einsum(
        "rkgn,rkgd->nkd", prob_low, grad_out, preferred_element_type=jnp.float32
    )
    return (output, grad_query, grad_keys, grad_values)


def on_device(queries, grad_attended, vision, key_weight, value_weight, tile_limit):
    halves = jnp.stack([key_weight[0], value_weight[0]], axis=0)
    partner = from_partner(halves, "segment", 0)
    segment_index = lax.axis_index("segment")
    holds_first = segment_index % 2 == 0
    first_rows = jnp.where(holds_first, halves, partner)
    second_rows = jnp.where(holds_first, partner, halves)
    full_weights = jnp.concatenate([first_rows, second_rows], axis=1)
    key_matrix = full_weights[0]
    value_matrix = full_weights[1]
    joined_weights = jnp.concatenate([key_matrix, value_matrix], axis=1)
    kv_width = key_matrix.shape[1]
    kv_local = kv_width // HD
    heads_local = queries.shape[2] // HD
    group = heads_local // kv_local
    rows_dev = vision.shape[0]
    vis_total = rows_dev * lax.axis_size("segment")
    tile_tokens = vis_total // TILES
    text_rows = queries.shape[1]
    limit_start = segment_index % 2 * text_rows
    own_limits = lax.dynamic_slice_in_dim(tile_limit, limit_start, text_rows, 0)
    widened = lax.all_gather(vision, "tensor", axis=1, tiled=True)
    projected = jnp.dot(
        lax.all_gather(widened, "segment", axis=0, tiled=True),
        joined_weights,
        preferred_element_type=jnp.float32,
    )
    key_pre = projected[:, :kv_width].reshape(vis_total, kv_local, HD)
    keys = normalize(key_pre).astype(jnp.bfloat16)
    values = projected[:, kv_width:].reshape(vis_total, kv_local, HD).astype(jnp.bfloat16)
    block_rows = min(512, text_rows)
    query_block = queries[0, 0:block_rows].reshape(block_rows, kv_local, group, HD)
    grad_block = grad_attended[0, 0:block_rows].reshape(block_rows, kv_local, group, HD)
    output, grad_query, block_keys, block_values = attend(
        query_block, grad_block, keys, values, own_limits, tile_tokens
    )
    outputs = output.reshape(block_rows, heads_local * HD)
    query_grads = grad_query.reshape(block_rows, heads_local * HD)
    attended = outputs[None]
    grad_queries = query_grads[None]
    grad_pre = jax.vjp(normalize, key_pre)[1](block_keys)[0]
    grad_pre = grad_pre.astype(jnp.bfloat16).reshape(vis_total, kv_width)
    grad_vals = block_values.astype(jnp.bfloat16).reshape(vis_total, kv_width)
    term = jnp.dot(grad_pre, key_matrix.T, preferred_element_type=jnp.float32)
    row_part = lax.psum_scatter(
        (term + jnp.dot(grad_vals, value_matrix.T, preferred_element_type=jnp.float32)).astype(
            jnp.bfloat16
        ),
        "segment",
        scatter_dimension=0,
        tiled=True,
    )
    grad_vision = lax.psum_scatter(row_part, "tensor", scatter_dimension=1, tiled=True).astype(
        jnp.float32
    )
    return (attended, grad_queries, grad_vision)


def solution(mesh):
    return jax.shard_map(
        on_device,
        mesh=mesh,
        in_specs=(
            P("segment", None, "tensor"),
            P("segment", None, "tensor"),
            P("segment", "tensor"),
            P("segment", None, "tensor"),
            P("segment", None, "tensor"),
            P(),
        ),
        out_specs=(
            P("segment", None, "tensor"),
            P("segment", None, "tensor"),
            P("segment", "tensor"),
        ),
        check_vma=False,
    )
```

profile of v0, /device:TPU:1, one launch (start us, length us, event | category | flops | bytes accessed | tf_op | source)
XLA Modules:
  0.0 316.7 jit_solution(2021049578270759455)
XLA Ops:
  7.2 0.0 copy-start.5
  7.2 0.0 copy-start.8
  7.2 0.0 all-gather.2.cloned.1.call-start
  7.2 26.7 %all_gather.6 = bf16[16,8192]{1,0:T(8,128)(2,1)} all-gather(bf16[16,1024]{1,0:T(8,128)(2,1)} %param.8), channel_id=1, replica_groups=mesh['segment'=32,'tensor'=8] {'tensor'}, dimensions={1}, use_global_device_ids=true | all-gather | bytes 294912 | tf_op jit(solution)/shard_map/all_gather | solution.py:78
  34.0 0.0 all-gather.2.cloned.1.call-update
  34.0 0.0 reduce-scatter.3.cloned.1.call-start
  34.0 1.3 constant_dynamic-update-slice_fusion.1
  35.3 1.4 constant_dynamic-update-slice_fusion
  36.7 7.9 %collective-permute-start = (bf16[2,4096,128]{2,1,0:T(8,128)(2,1)S(1)}, bf16[2,4096,128]{2,1,0:T(8,128)(2,1)}, u32[]{:S(2)}, u32[]{:S(2)}) collective-permute-start(bf16[2,4096,128]{2,1,0:T(8,128)(2,1)S(1)} %constant_dynamic-update-slice_fusion), channel_id=1, source_target_pairs={{0,8},{8,0},{16,24},{24,16},{32,40},{40,32},{48,56},{56,48},{64,72... | collective-permute-start | bytes 6291464 | tf_op jit(solution)/shard_map/ppermute | solution.py:16
  44.6 1.2 copy.27
  45.9 0.0 copy-done.5
  45.9 1.2 copy.14
  47.0 0.9 copy.28
  47.9 0.0 copy-done.8
  47.9 0.1 dynamic-slice_multiply_fusion
  48.0 0.1 iota_compare_fusion
  48.1 0.4 collective-permute-done
  48.5 1.9 broadcast_select_fusion.1
  50.4 8.3 %fusion.9 = (bf16[8192,128]{1,0:T(8,128)(2,1)}, bf16[8192,128]{1,0:T(8,128)(2,1)S(1)}) fusion(bf16[2,4096,128]{2,1,0:T(8,128)(2,1)S(1)} %get-tuple-element.8, bf16[2,4096,128]{2,1,0:T(8,128)(2,1)S(1)} %get-tuple-element.9), kind=kLoop, calls=%fused_computation.16 | loop fusion | flops 8388608 | bytes 8388608 | tf_op jit(solution)/shard_map/squeeze | solution.py:65
  58.7 59.6 %all-gather.2.cloned.1.call-done = bf16[512,8192]{1,0:T(8,128)(2,1)} async-done(((bf16[16,8192]{1,0:T(8,128)(2,1)}), bf16[512,8192]{1,0:T(8,128)(2,1)}) %all-gather.2.cloned.1.call-update) | async-done | bytes 8388624 | tf_op jit(solution)/shard_map/all_gather | solution.py:80
  118.3 6.4 %fusion.29 = f32[512,256]{0,1:T(8,128)S(1)} fusion(bf16[512,8192]{1,0:T(8,128)(2,1)} %all-gather.2.cloned.1.call-done, bf16[8192,128]{1,0:T(8,128)(2,1)S(1)} %get-tuple-element.7, bf16[8192,128]{1,0:T(8,128)(2,1)} %get-tuple-element.6), kind=kOutput, calls=%fused_computation.33 | convolution fusion | flops 2155872256 | bytes 13107200 | tf_op jit(solution)/shard_map/dot_general | solution.py:79
  124.7 0.0 copy-done.1
  124.8 0.0 copy-start.6
  124.8 0.8 fusion.7
  125.7 0.0 copy-start
  125.7 0.9 fusion.6
  126.5 0.0 copy-done.6
  126.6 0.0 copy-start.3
  126.6 2.2 multiply_reduce_fusion
  128.7 0.0 copy-done
  128.7 0.0 copy-done.3
  128.7 1.5 fusion.4
  130.3 0.0 copy-start.2
  130.3 0.8 fusion.47
  131.1 0.7 copy-done.2
  131.9 8.1 %fusion.51 = f32[512,8192]{1,0:T(8,128)} fusion(bf16[8192,128]{1,0:T(8,128)(2,1)S(1)} %copy-done.2, f32[512,256]{0,1:T(8,128)S(1)} %fusion.29, f32[1,128,512]{2,1,0:T(8,128)S(1)} %get-tuple-element.17, f32[512]{0:T(512)S(1)} %get-tuple-element.11, f32[512]{0:T(512)S(1)} %get-tuple-element.10), kind=kOutput, calls=%fused_computation.51 | convolution fusion | flops 1074069504 | bytes 19402752 | tf_op jit(solution)/shard_map/dot_general | solution.py:100
  140.0 0.0 copy-done.4
  140.0 11.6 %add_convert_fusion = bf16[512,8192]{1,0:T(8,128)(2,1)} fusion(f32[512,8192]{1,0:T(8,128)} %fusion.51, bf16[8192,128]{1,0:T(8,128)(2,1)} %copy-done.1, bf16[256,8,128]{2,1,0:T(8,128)(2,1)S(1)} %bitcast.134, f32[256,8]{0,1:T(8,128)S(1)} %fusion.6, f32[256,8]{0,1:T(8,128)S(1)} %get-tuple-element.12, f32[512,256,8]{1,0,2:T(8,128)} %copy-done, ...), kind=kOutput, calls=%fused_computation | convolution fusion | flops 1355874304 | bytes 32129024 | tf_op jit(solution)/shard_map/dot_general | solution.py:102
  151.7 0.0 reduce-scatter.3.cloned.1.call-update
  151.7 0.0 reduce-scatter.5.cloned.1.call-start
  151.7 121.4 %reduce-scatter.3.cloned.1.call-done = bf16[16,8192]{1,0:T(8,128)(2,1)} async-done(((bf16[512,8192]{1,0:T(8,128)(2,1)}), bf16[16,8192]{1,0:T(8,128)(2,1)}) %reduce-scatter.3.cloned.1.call-update) | async-done | bytes 262160 | tf_op jit(solution)/shard_map/reduce_scatter | solution.py:101
  273.1 0.0 reduce-scatter.5.cloned.1.call-update
  273.1 0.0 copy-done.7
  273.2 1.0 copy.18
  274.2 0.5 fusion.23
  274.6 1.0 copy.19
  275.6 33.2 %reduce-scatter.5.cloned.1.call-done = bf16[16,1024]{1,0:T(8,128)(2,1)} async-done(((bf16[16,8192]{1,0:T(8,128)(2,1)}), bf16[16,1024]{1,0:T(8,128)(2,1)}) %reduce-scatter.5.cloned.1.call-update) | async-done | bytes 32784 | tf_op jit(solution)/shard_map/reduce_scatter | solution.py:109
  308.8 1.4 convert_element_type.77
  (6 shorter events, 0.1 us)
Async XLA Ops:
  7.2 38.7 %copy-start.5 = (bf16[1,256,1024]{2,1,0:T(8,128)(2,1)S(1)}, bf16[1,256,1024]{2,1,0:T(8,128)(2,1)}, u32[]{:S(2)}) copy-start(bf16[1,256,1024]{2,1,0:T(8,128)(2,1)} %param.7) | copy-start | bytes 1572868
  7.2 40.8 %copy-start.8 = (s32[512]{0:T(512)S(1)}, s32[512]{0:T(512)}, u32[]{:S(2)}) copy-start(s32[512]{0:T(512)} %param.11) | copy-start | bytes 6148
  7.2 111.1 %all-gather.2.cloned.1.call-start = ((), (), s32[]{:S(2)}) async-start(), calls=%async_computation.2 | async-start | bytes 8650752 | tf_op jit(solution)/shard_map/all_gather | solution.py:80
  34.0 239.1 %reduce-scatter.3.cloned.1.call-start = ((), (), s32[]{:S(2)}) async-start(), calls=%async_computation.3 | async-start | bytes 8650752 | tf_op jit(solution)/shard_map/reduce_scatter | solution.py:101
  36.7 11.8 %collective-permute-start = (bf16[2,4096,128]{2,1,0:T(8,128)(2,1)S(1)}, bf16[2,4096,128]{2,1,0:T(8,128)(2,1)}, u32[]{:S(2)}, u32[]{:S(2)}) collective-permute-start(bf16[2,4096,128]{2,1,0:T(8,128)(2,1)S(1)} %constant_dynamic-update-slice_fusion), channel_id=1, source_target_pairs={{0,8},{8,0},{16,24},{24,16},{32,40},{40,32},{48,56},{56,48},{64,72... | collective-permute-start | bytes 6291464 | tf_op jit(solution)/shard_map/ppermute | solution.py:16
  58.7 66.1 %copy-start.1 = (bf16[8192,128]{1,0:T(8,128)(2,1)}, bf16[8192,128]{1,0:T(8,128)(2,1)S(1)}, u32[]{:S(2)}) copy-start(bf16[8192,128]{1,0:T(8,128)(2,1)S(1)} %get-tuple-element.7) | copy-start | bytes 6291460
  124.8 1.8 copy-start.6
  125.7 3.1 copy-start
  126.6 2.2 copy-start.3
  130.3 1.6 copy-start.2
  131.9 8.1 %copy-start.4 = (bf16[32,8,8,128]{3,2,1,0:T(8,128)(2,1)S(1)}, bf16[32,8,8,128]{3,2,1,0:T(8,128)(2,1)}, u32[]{:S(2)}) copy-start(bf16[32,8,8,128]{3,2,1,0:T(8,128)(2,1)} %copy.28) | copy-start | bytes 1572868
  151.7 121.5 %copy-start.7 = (bf16[128,256,8]{1,0,2:T(8,128)(2,1)S(1)}, bf16[128,256,8]{1,0,2:T(8,128)(2,1)}, u32[]{:S(2)}) copy-start(bf16[128,256,8]{1,0,2:T(8,128)(2,1)} %get-tuple-element.15) | copy-start | bytes 1572868
  151.7 157.1 %reduce-scatter.5.cloned.1.call-start = ((), (), s32[]{:S(2)}) async-start(), calls=%async_computation.4 | async-start | bytes 294912 | tf_op jit(solution)/shard_map/reduce_scatter | solution.py:109
Sparse Core Ops, SparseCore 0:
  34.1 84.1 all-gather.1
  151.8 121.2 reduce-scatter.2
  275.8 32.9 reduce-scatter.4
where the time goes:
time: 321 us; the launch traced here: 317 us
  waiting for transfers between devices  215 us (67%)
  matrix products  32 us (10%)
  blocking collectives  26.7 us (8%)
  between operations  13.9 us (4%)
  other arithmetic  12.6 us (4%)
  local copies, waits for them, and re-layouts  8.76 us (3%)
  starting transfers between devices  8.02 us (2%)
    reduce_scatter x1, waiting for transfers between devices, on_device(): lax.psum_scatter((term + jnp.dot(grad_vals, value_matrix.T, preferred_ele...  121 us
    all_gather x1, waiting for transfers between devices, on_device(): lax.all_gather(widened, 'segment', axis=0, tiled=True)  59.6 us
    reduce_scatter x1, waiting for transfers between devices, on_device(): lax.psum_scatter(row_part, 'tensor', scatter_dimension=1, tiled=True)  33.2 us
    all_gather x1, blocking collectives, on_device(): widened = lax.all_gather(vision, 'tensor', axis=1, tiled=True)  26.7 us
    dot_general x1, matrix products, on_device(): jnp.dot(grad_vals, value_matrix.T, preferred_element_type=jnp.float32)  11.6 us
    squeeze x1, other arithmetic, on_device(): key_matrix = full_weights[0]  8.28 us
    dot_general x1, matrix products, on_device(): term = jnp.dot(grad_pre, key_matrix.T, preferred_element_type=jnp.float32)  8.12 us
    ppermute x1, starting transfers between devices, from_partner(): return lax.ppermute(value, axis, pairs)  7.89 us
  transfers between devices with their start and end apart: 4, of which 4 were waited for; matrix products, arithmetic and copies ran while one was open for 6% of the time, Pallas kernels for 0%

commit v1 on v0

v1 whole, which is shorter than its diff:
```python
import jax
import jax.numpy as jnp
from jax import lax
from jax.experimental import pallas as pl
from jax.experimental.pallas import tpu as pltpu
from jax.sharding import PartitionSpec as P

HD = 128
EPS = 1e-05
SCALE = HD ** (-0.5)
LOG2E = 1.4426950408889634
F32 = jnp.float32
BF16 = jnp.bfloat16
MESH = pl.DeviceIdType.MESH


def dot(a, b):
    return jnp.dot(a, b, preferred_element_type=F32)


def kernel(
    vis, wk, wv, q, do, lim, att_o, dq_o, gv_o,
    g, pb, w, wt, qt, dot_, bias, part, part_in, kv, kvt, dkv, dkv_in, acc,
    r1o, r1n, r1yo, r1yn, sx, sy, r2x, r2y, tx, ty, r3,
    ss1, rs1, ss2, rs2x, rs2y, ss3, rs3x, rs3y, ss4, rs4, lsem,
    ssr1, rsr1x, rsr1y, ssr2, rsr2x, rsr2y, ssr3, rsr3,
):
    seg, ten = lax.axis_index("segment"), lax.axis_index("tensor")
    zh, x, c = lax.div(seg, 8), lax.rem(lax.div(seg, 2), 4), lax.rem(seg, 2)
    y, zl = lax.div(ten, 2), lax.rem(ten, 2)
    z = zh * 2 + zl
    zi = zl * 4 + zh
    h, yp = lax.div(y, 2), lax.rem(y, 2)
    role = lax.rem(y + 4 - 2 * c, 4)
    home = c == h

    def dev(xx, yy, zz, cc):
        return (lax.div(zz, 2) * 8 + xx * 2 + cc, yy * 2 + lax.rem(zz, 2))

    def zind(zz):
        return lax.rem(zz, 2) * 4 + lax.div(zz, 2)

    def xo(d):
        return lax.rem(x + d + 4, 4)

    def yo(d):
        return lax.rem(y + d + 4, 4)

    def zo(d):
        return lax.rem(z + d + 8, 8)

    partner = dev(x, y, z, 1 - c)

    def rdma(src, dst, ss, rs, to):
        return pltpu.make_async_remote_copy(
            src_ref=src, dst_ref=dst, send_sem=ss, recv_sem=rs, device_id=to, device_id_type=MESH
        )

    def arrived(dst, rs):
        rdma(dst, dst, ss4.at[0], rs, partner).wait_recv()

    wcopies = [
        pltpu.make_async_copy(wk.at[0], w.at[:, pl.ds(0, HD)], lsem.at[0]),
        pltpu.make_async_copy(wv.at[0], w.at[:, pl.ds(HD, HD)], lsem.at[1]),
    ]
    for cp in wcopies:
        cp.start()

    barrier = pltpu.get_barrier_semaphore()
    greet = [dev(x, y, zo(d), cc) for d in range(1, 8) for cc in (0, 1)]
    greet += [dev(xo(d), y, z, c) for d in range(1, 4)]
    greet += [dev(x, yo(d), z, c) for d in range(1, 4)] + [partner]
    for other in greet:
        pl.semaphore_signal(barrier, inc=1, device_id=other, device_id_type=MESH)
    pl.semaphore_wait(barrier, len(greet))

    mine = (1 - c) * (x * 2 + yp) + c * (yp * 4 + x)

    def g1(d):
        return rdma(vis, g.at[c, mine, zi], ss1.at[d], rs1.at[c, zi], dev(x, y, zo(d), h))

    def g1_local():
        return pltpu.make_async_copy(vis, g.at[c, mine, zi], rs1.at[c, zi])

    for d in (4, 3, 5, 2, 6, 1, 7):
        g1(d).start()

    @pl.when(home)
    def _():
        g1_local().start()

    @pl.when(c == 1 - h)
    def _():
        g1(0).start()

    @pl.loop(0, 8)
    def _(n):
        lanes = pl.ds(pl.multiple_of(n * HD, HD), HD)
        qt[n] = q[0, :, lanes].astype(F32).T.astype(BF16)
        dot_[n] = do[0, :, lanes].astype(F32).T.astype(BF16)

    limit = (1 - c) * lim[0:1, :] + c * lim[1:2, :]
    for t in range(4):
        bias[t] = jnp.broadcast_to(jnp.where(t < limit, 0.0, -1e30), (16, 256))

    def g2x(d):
        blk = g.at[0, x * 2 + yp]
        return rdma(blk, blk, ss2.at[0, d], rs2x.at[yp], dev(x, yo(d), z, c))

    def g2y(d):
        blk = g.at[1, yp * 4 + x]
        return rdma(blk, blk, ss2.at[1, d], rs2y.at[x], dev(xo(d), y, z, c))

    @pl.when(home)
    def _():
        for zz in range(8):
            arrived(g.at[0, x * 2 + yp, zz], rs1.at[0, zz])
        for d in (2, 1, 3):
            g2x(d).start()
        for zz in range(8):
            arrived(g.at[1, yp * 4 + x, zz], rs1.at[1, zz])
        for d in (2, 1, 3):
            g2y(d).start()

    for cp in wcopies:
        cp.wait()

    @pl.loop(0, 16)
    def _(n):
        rows = pl.ds(pl.multiple_of(n * 256, 256), 256)
        wt[:, rows] = w[rows, :].astype(F32).T.astype(BF16)

    def g3x(d, half):
        blk = g.at[0, x * 2 + half]
        return rdma(blk, blk, ss3.at[0, d, half], rs3x.at[d, half], dev(xo(1 - 2 * d), y, z, c))

    def g3xf(d):
        blk = g.at[0, xo(2 * d - 1) * 2 + d]
        return rdma(blk, blk, ss3.at[0, d, 2], rs3x.at[d, 2], dev(xo(1 - 2 * d), y, z, c))

    def ywait_x(k):
        @pl.when(jnp.logical_not(jnp.logical_and(home, yp == k)))
        def _():
            arrived(g.at[0, x * 2 + k], rs2x.at[k])

    for k in range(2):
        ywait_x(k)
    for d, half in ((0, 0), (1, 1), (0, 1), (1, 0)):
        g3x(d, half).start()

    def half_y(k, j):
        return pl.ds(k * 4 + j * 2, 2)

    def g3y(k, j, d):
        blk = g.at[1, half_y(k, j)]
        return rdma(blk, blk, ss3.at[1, d, j], rs3y.at[k, j], dev(x, yo(1 - 2 * d), z, c))

    def g3y_role(r):
        if r == 0:
            return [g3y(0, 0, 0), g3y(0, 1, 1), g3y(0, 1, 0), g3y(0, 0, 1)]
        return [g3y(1, 0, 1), g3y(1, 1, 0), g3y(1, 1, 1), g3y(1, 0, 0)]

    def g3yf(r):
        k, j, d = ((1, 0, 1), (0, 0, 0), (1, 1, 0), (0, 1, 1))[r]
        blk = g.at[1, half_y(k, j)]
        return rdma(blk, blk, ss3.at[1, d, 2], rs3y.at[k, j], dev(x, yo(1 - 2 * d), z, c))

    for r in (0, 1):
        @pl.when(role == r)
        def _():
            for d in range(1, 4):
                arrived(g.at[1, r * 4 + xo(d)], rs2y.at[xo(d)])
            for cp in g3y_role(r):
                cp.start()

    arrived(g.at[0, xo(-1) * 2], rs3x.at[0, 0])
    g3xf(0).start()
    arrived(g.at[0, xo(1) * 2 + 1], rs3x.at[1, 1])
    g3xf(1).start()
    for r in range(4):
        @pl.when(role == r)
        def _():
            k, j, _d = ((1, 0, 1), (0, 0, 0), (1, 1, 0), (0, 1, 1))[r]
            arrived(g.at[1, half_y(k, j)], rs3y.at[k, j])
            g3yf(r).start()

    arrived(g.at[0, xo(-1) * 2 + 1], rs3x.at[0, 1])
    arrived(g.at[0, xo(1) * 2], rs3x.at[1, 0])
    arrived(g.at[0, xo(2) * 2], rs3x.at[0, 2])
    arrived(g.at[0, xo(2) * 2 + 1], rs3x.at[1, 2])
    for r in range(4):
        @pl.when(role == r)
        def _():
            first = ((1, 0), (0, 0), (1, 1), (0, 1))[r]
            for k in (0, 1):
                if r == k:
                    continue
                for j in (0, 1):
                    if (k, j) != first:
                        arrived(g.at[1, half_y(k, j)], rs3y.at[k, j])

    for p in range(2):
        total = jnp.zeros((256, 2 * HD), F32)
        for k in range(2):
            for l in range(2):
                if p == 0:
                    a = jnp.concatenate(
                        [g[0, xx * 2 + k, l * 4 : l * 4 + 4].reshape(64, 1024) for xx in range(4)], axis=0
                    )
                else:
                    a = g[1, k * 4 : k * 4 + 4, l * 4 : l * 4 + 4].reshape(256, 1024)
                base = (k * 2 + l) * 1024
                total += dot(a, w[base : base + 1024, :])
        part[p * 256 : (p + 1) * 256, :] = total

    swap = rdma(part, part_in, ss4.at[0], rs4.at[0], partner)
    swap.start()
    swap.wait()
    pre = part[...] + part_in[...]
    part[...] = pre
    kp = pre[:, :HD]
    inv = lax.rsqrt(jnp.mean(kp * kp, axis=-1, keepdims=True) + EPS)
    keys = kp * inv
    vals = pre[:, HD:]
    kv[0] = keys.astype(BF16)
    kv[1] = vals.astype(BF16)
    kvt[0] = keys.astype(BF16).astype(F32).T.astype(BF16)
    kvt[1] = vals.astype(BF16).astype(F32).T.astype(BF16)

    acc[...] = jnp.zeros_like(acc)

    @pl.loop(0, 8)
    def _(n):
        lanes = pl.ds(pl.multiple_of(n * HD, HD), HD)
        qn = q[0, :, lanes]
        don = do[0, :, lanes]
        dotn = dot_[n]
        s = dot(kv[0], qt[n]) * (SCALE * LOG2E)
        s = (s.reshape(8, 4, 16, 256) + bias[...][None]).reshape(512, 256)
        m = jnp.max(s, axis=0, keepdims=True)
        e = jnp.exp2(s - m)
        prob = e * (1.0 / jnp.sum(e, axis=0, keepdims=True))
        pb16 = prob.astype(BF16)
        at = dot(kvt[1], pb16).astype(BF16).astype(F32)
        dp = dot(kv[1], dotn)
        delta = jnp.sum(at * dotn.astype(F32), axis=0, keepdims=True)
        ds = (prob * (dp - delta)).astype(BF16)
        att_o[0, :, lanes] = at.T.astype(BF16)
        dqt = dot(kvt[0], ds) * SCALE
        dq_o[0, :, lanes] = dqt.T.astype(BF16)
        acc[0] += dot(ds, qn)
        acc[1] += dot(pb16, don)

    kp = part[:, :HD]
    inv = lax.rsqrt(jnp.mean(kp * kp, axis=-1, keepdims=True) + EPS)
    dk = acc[0] * SCALE
    dkp = inv * dk - kp * (inv * inv * inv * jnp.mean(kp * dk, axis=-1, keepdims=True))
    dkv[:, :HD] = dkp.astype(BF16)
    dkv[:, HD:] = acc[1].astype(BF16)
    swap2 = rdma(dkv, dkv_in, ss4.at[1], rs4.at[1], partner)
    swap2.start()
    swap2.wait()

    for k in range(2):
        for l in range(2):
            base = (k * 2 + l) * 1024
            for p in range(2):
                rows = slice(p * 256, (p + 1) * 256)
                wtb = wt[:, base : base + 1024]
                v = (dot(dkv[rows, :], wtb) + dot(dkv_in[rows, :], wtb)).astype(BF16)
                if p == 0:
                    for xx in range(4):
                        pb[0, xx * 2 + k, l * 4 : l * 4 + 4] = v[xx * 64 : (xx + 1) * 64].reshape(4, 16, 1024)
                else:
                    pb[1, k * 4 : k * 4 + 4, l * 4 : l * 4 + 4] = v.reshape(4, 4, 16, 1024)

    def r1x_opp(d):
        return rdma(pb.at[0, xo(2) * 2 + d], r1o.at[d], ssr1.at[0, d], rsr1x.at[0, d], dev(xo(1 - 2 * d), y, z, c))

    def r1x_free(d):
        return rdma(
            pb.at[0, xo(1 - 2 * d) * 2 + 1 - d], r1n.at[d, 1 - d], ssr1.at[0, 2 + d], rsr1x.at[1, d],
            dev(xo(1 - 2 * d), y, z, c),
        )

    def r1x_dep(d):
        return rdma(
            pb.at[0, xo(1 - 2 * d) * 2 + d], r1n.at[d, d], ssr1.at[0, 4 + d], rsr1x.at[2, d],
            dev(xo(1 - 2 * d), y, z, c),
        )

    y_opp = {2: ((1, 0, 0), (0, 0, 1)), 3: ((0, 1, 0), (1, 1, 1))}
    y_free = {0: (0, 1, 1), 1: (1, 0, 1), 2: (1, 1, 0), 3: (0, 0, 0)}
    y_dep = {0: (0, 1, 0), 1: (1, 0, 0), 2: (1, 1, 1), 3: (0, 0, 1)}

    def r1y_opp(r, i):
        d, k, j = y_opp[r][i]
        return rdma(pb.at[1, half_y(k, j)], r1yo, ssr1.at[1, i], rsr1y.at[0], dev(x, yo(1 - 2 * d), z, c))

    def r1y_free(r):
        d, k, j = y_free[r]
        side = 0 if r >= 2 else 1
        return rdma(
            pb.at[1, half_y(k, j)], r1yn.at[side, pl.ds(j * 2, 2)], ssr1.at[1, 2], rsr1y.at[1 + side * 2],
            dev(x, yo(1 - 2 * d), z, c),
        )

    def r1y_dep(r):
        d, k, j = y_dep[r]
        side = 0 if r >= 2 else 1
        return rdma(
            pb.at[1, half_y(k, j)], r1yn.at[side, pl.ds(j * 2, 2)], ssr1.at[1, 3], rsr1y.at[2 + side * 2],
            dev(x, yo(1 - 2 * d), z, c),
        )

    for d in range(2):
        r1x_opp(d).start()
    for r in (2, 3):
        @pl.when(role == r)
        def _():
            for i in range(2):
                r1y_opp(r, i).start()
    for d in range(2):
        r1x_free(d).start()
    for r in range(4):
        @pl.when(role == r)
        def _():
            r1y_free(r).start()

    def add_into(dst, src, n):
        @pl.loop(0, n)
        def _(i):
            dst(i)[...] = (dst(i)[...].astype(F32) + src(i)[...].astype(F32)).astype(BF16)

    for d in range(2):
        arrived(r1o.at[d], rsr1x.at[0, d])
        to = xo(1 - 2 * d) * 2 + d
        add_into(lambda i: pb.at[0, to, i], lambda i: r1o.at[d, i], 8)
        r1x_dep(d).start()
    arrived(r1yo, rsr1y.at[0])
    for r in range(4):
        @pl.when(role == r)
        def _():
            _d, k, j = y_dep[r]
            add_into(
                lambda i: pb.at[1, k * 4 + j * 2 + lax.div(i, 8), lax.rem(i, 8)],
                lambda i: r1yo.at[lax.div(i, 8), lax.rem(i, 8)],
                16,
            )
            r1y_dep(r).start()

    for d in range(2):
        arrived(r1n.at[d, 1 - d], rsr1x.at[1, d])
    for d in range(2):
        arrived(r1n.at[d, d], rsr1x.at[2, d])

    @pl.loop(0, 16)
    def _(i):
        k, b = lax.div(i, 8), lax.rem(i, 8)
        sx[k, b] = (pb[0, x * 2 + k, b].astype(F32) + r1n[0, k, b].astype(F32) + r1n[1, k, b].astype(F32)).astype(BF16)

    def r2x_to(k):
        return rdma(sx.at[k], r2x.at[y], ssr2.at[0, k], rsr2x.at[y], dev(x, 2 * c + k, z, c))

    def r2y_to(d):
        return rdma(sy.at[xo(d)], r2y.at[x], ssr2.at[1, d], rsr2y.at[x], dev(xo(d), y, z, c))

    for k in range(2):
        @pl.when(role != k)
        def _():
            r2x_to(k).start()

    @pl.when(home)
    def _():
        arrived(r1yn.at[0, pl.ds(0, 2)], rsr1y.at[1])
        arrived(r1yn.at[1, pl.ds(2, 2)], rsr1y.at[3])
        arrived(r1yn.at[0, pl.ds(2, 2)], rsr1y.at[2])
        arrived(r1yn.at[1, pl.ds(0, 2)], rsr1y.at[4])

        @pl.loop(0, 32)
        def _(i):
            k, b = lax.div(i, 8), lax.rem(i, 8)
            sy[k, b] = (
                pb[1, yp * 4 + k, b].astype(F32) + r1yn[0, k, b].astype(F32) + r1yn[1, k, b].astype(F32)
            ).astype(BF16)

        for d in (2, 1, 3):
            r2y_to(d).start()

        for d in range(1, 4):
            arrived(r2x.at[yo(d)], rsr2x.at[yo(d)])

        @pl.loop(0, 8)
        def _(b):
            v = sx[yp, b].astype(F32)
            for d in range(1, 4):
                v += r2x[yo(d), b].astype(F32)
            tx[b] = v.astype(BF16)

    def r3_to(t, cc, d):
        zz = zo(d)
        return rdma(t.at[zind(zz)], r3.at[zi], ssr3.at[cc, d], rsr3.at[zi], dev(x, y, zz, cc))

    def r3_all(t, cc, act):
        for d in (4, 3, 5, 2, 6, 1, 7):
            act(r3_to(t, cc, d))

        @pl.when(c != cc)
        def _():
            act(r3_to(t, cc, 0))

    def r3_local(t):
        return pltpu.make_async_copy(t.at[zi], r3.at[zi], rsr3.at[zi])

    def begin(cp):
        cp.start()

    @pl.when(home)
    def _():
        r3_all(tx, 0, begin)

        @pl.when(c == 0)
        def _():
            r3_local(tx).start()

        for d in range(1, 4):
            arrived(r2y.at[xo(d)], rsr2y.at[xo(d)])

        @pl.loop(0, 8)
        def _(b):
            v = sy[x, b].astype(F32)
            for d in range(1, 4):
                v += r2y[xo(d), b].astype(F32)
            ty[b] = v.astype(BF16)

        r3_all(ty, 1, begin)

        @pl.when(c == 1)
        def _():
            r3_local(ty).start()

    for b in range(8):
        arrived(r3.at[b], rsr3.at[b])
    total = r3[0].astype(F32)
    for b in range(1, 8):
        total += r3[b].astype(F32)
    gv_o[...] = total

    def sent(cp):
        cp.wait_send()

    for d in range(1, 8):
        sent(g1(d))

    @pl.when(c == 1 - h)
    def _():
        sent(g1(0))

    @pl.when(home)
    def _():
        for d in range(1, 4):
            sent(g2x(d))
            sent(g2y(d))
            sent(r2y_to(d))
        r3_all(tx, 0, sent)
        r3_all(ty, 1, sent)

    for d in range(2):
        for half in range(2):
            sent(g3x(d, half))
        sent(g3xf(d))
        sent(r1x_opp(d))
        sent(r1x_free(d))
        sent(r1x_dep(d))
    for r in range(4):
        @pl.when(role == r)
        def _():
            if r < 2:
                for cp in g3y_role(r):
                    sent(cp)
            else:
                for i in range(2):
                    sent(r1y_opp(r, i))
            sent(g3yf(r))
            sent(r1y_free(r))
            sent(r1y_dep(r))
    for k in range(2):
        @pl.when(role != k)
        def _():
            sent(r2x_to(k))


def on_device(queries, grad_attended, vision, key_weight, value_weight, tile_limit):
    vmem = pl.BlockSpec(memory_space=pltpu.VMEM)
    hbm = pl.BlockSpec(memory_space=pl.ANY)
    dma = pltpu.SemaphoreType.DMA
    return pl.pallas_call(
        kernel,
        out_shape=(
            jax.ShapeDtypeStruct(queries.shape, BF16),
            jax.ShapeDtypeStruct(queries.shape, BF16),
            jax.ShapeDtypeStruct(vision.shape, F32),
        ),
        in_specs=[vmem, hbm, hbm, vmem, vmem, vmem],
        out_specs=(vmem, vmem, vmem),
        scratch_shapes=[
            pltpu.VMEM((2, 8, 8, 16, 1024), BF16),
            pltpu.VMEM((2, 8, 8, 16, 1024), BF16),
            pltpu.VMEM((4096, 256), BF16),
            pltpu.VMEM((256, 4096), BF16),
            pltpu.VMEM((8, 128, 256), BF16),
            pltpu.VMEM((8, 128, 256), BF16),
            pltpu.VMEM((4, 16, 256), F32),
            pltpu.VMEM((512, 256), F32),
            pltpu.VMEM((512, 256), F32),
            pltpu.VMEM((2, 512, 128), BF16),
            pltpu.VMEM((2, 128, 512), BF16),
            pltpu.VMEM((512, 256), BF16),
            pltpu.VMEM((512, 256), BF16),
            pltpu.VMEM((2, 512, 128), F32),
            pltpu.VMEM((2, 8, 16, 1024), BF16),
            pltpu.VMEM((2, 2, 8, 16, 1024), BF16),
            pltpu.VMEM((2, 8, 16, 1024), BF16),
            pltpu.VMEM((2, 4, 8, 16, 1024), BF16),
            pltpu.VMEM((2, 8, 16, 1024), BF16),
            pltpu.VMEM((4, 8, 16, 1024), BF16),
            pltpu.VMEM((4, 8, 16, 1024), BF16),
            pltpu.VMEM((4, 8, 16, 1024), BF16),
            pltpu.VMEM((8, 16, 1024), BF16),
            pltpu.VMEM((8, 16, 1024), BF16),
            pltpu.VMEM((8, 16, 1024), BF16),
            dma((8,)), dma((2, 8)),
            dma((2, 4)), dma((2,)), dma((4,)),
            dma((2, 2, 3)), dma((2, 3)), dma((2, 2)),
            dma((2,)), dma((2,)), dma((2,)),
            dma((2, 6)), dma((3, 2)), dma((5,)),
            dma((2, 4)), dma((4,)), dma((4,)),
            dma((2, 8)), dma((8,)),
        ],
        compiler_params=pltpu.CompilerParams(
            collective_id=0, has_side_effects=True, vmem_limit_bytes=52 * 2**20
        ),
        cost_estimate=pl.CostEstimate(flops=6_000_000_000, bytes_accessed=6_000_000, transcendentals=1_000_000),
    )(vision, key_weight, value_weight, queries, grad_attended, tile_limit.reshape(2, 256))


def solution(mesh):
    return jax.shard_map(
        on_device,
        mesh=mesh,
        in_specs=(
            P("segment", None, "tensor"),
            P("segment", None, "tensor"),
            P("segment", "tensor"),
            P("segment", None, "tensor"),
            P("segment", None, "tensor"),
            P(),
        ),
        out_specs=(
            P("segment", None, "tensor"),
            P("segment", None, "tensor"),
            P("segment", "tensor"),
        ),
        check_vma=False,
    )
```

time: 321 us -> 107 us (0.33); the launches traced: 317 us -> 107 us
  waiting for transfers between devices: 215 us -> 0 us
  Pallas kernels: 0 us -> 102 us
  matrix products: 32 us -> 0 us
  blocking collectives: 26.7 us -> 0 us
  between operations: 13.9 us -> 0.64 us
  other arithmetic: 12.6 us -> 0 us
  starting transfers between devices: 8.02 us -> 0 us
  local copies, waits for them, and re-layouts: 8.76 us -> 4.71 us
    reduce_scatter x2 -> x0, waiting for transfers between devices: 155 us -> none  [the longest x1 121 us: on_device(): lax.psum_scatter((term + jnp.dot(grad_vals, value_matrix.T, preferred_ele...]
    pallas_call x0 -> x1, Pallas kernels: none -> 102 us  [on_device(): pl.pallas_call(kernel, out_shape=(jax.ShapeDtypeStruct(queries.shape, BF1...]
    all_gather x1 -> x0, waiting for transfers between devices: 59.6 us -> none  [on_device(): lax.all_gather(widened, 'segment', axis=0, tiled=True)]
    dot_general x8 -> x0, matrix products: 32 us -> none  [the longest x1 11.6 us: on_device(): jnp.dot(grad_vals, value_matrix.T, preferred_element_type=jnp.float32)]
    all_gather x1 -> x0, blocking collectives: 26.7 us -> none  [on_device(): widened = lax.all_gather(vision, 'tensor', axis=1, tiled=True)]
    squeeze x1 -> x0, other arithmetic: 8.28 us -> none  [on_device(): key_matrix = full_weights[0]]
    ppermute x1 -> x0, starting transfers between devices: 7.89 us -> none  [from_partner(): return lax.ppermute(value, axis, pairs)]
  transfers between devices with their start and end apart: 4 -> 0, of which waited for: 4 -> 0; matrix products, arithmetic and copies ran while one was open for 6% -> 0% of each run, Pallas kernels for 0% -> 0%
where the time goes in v1:
time: 107 us
  Pallas kernels  102 us (95%)
  local copies, waits for them, and re-layouts  4.71 us (4%)
    pallas_call x1, Pallas kernels, on_device(): pl.pallas_call(kernel, out_shape=(jax.ShapeDtypeStruct(queries.shape, BF1...  102 us
    unnamed x7, local copies, waits for them, and re-layouts  4.02 us

profile of v1, /device:TPU:1, one launch (start us, length us, event | category | flops | bytes accessed | tf_op | source)
XLA Modules:
  0.0 106.9 jit_solution(12777822257514078709)
XLA Ops:
  0.6 0.7 reshape.9.lim
  1.3 0.0 copy-start
  1.3 1.0 copy-done
  2.4 0.0 copy-start.1
  2.4 0.8 copy-done.1
  3.1 101.5 %shard_map.85 = (bf16[1,256,1024]{2,1,0:T(8,128)(2,1)S(1)}, bf16[1,256,1024]{2,1,0:T(8,128)(2,1)S(1)}, f32[16,1024]{1,0:T(8,128)S(1)}) custom-call(bf16[16,1024]{1,0:T(8,128)(2,1)S(1)} %copy-done.1, bf16[1,4096,128]{2,1,0:T(8,128)(2,1)} %wk.1, bf16[1,4096,128]{2,1,0:T(8,128)(2,1)} %wv.1, bf16[1,256,1024]{2,1,0:T(8,128)(2,1)S(1)} %copy-done, ...), custom_call_target="tpu_custom_call" | custom-call | flops 6000000000 | bytes 6000000 | tf_op jit(solution)/shard_map/pallas_call | solution.py:497
  104.7 0.8 copy.12
  105.5 0.8 copy.13
  106.2 0.6 copy.14
Async XLA Ops:
  1.3 1.0 copy-start
  2.4 0.8 copy-start.1

commit v2 on v0

v2 whole, which is shorter than its diff:
```python
import jax
import jax.numpy as jnp
from jax import lax
from jax.experimental import pallas as pl
from jax.experimental.pallas import tpu as pltpu
from jax.sharding import PartitionSpec as P

HD = 128
EPS = 1e-05
SCALE = HD ** (-0.5)
LOG2E = 1.4426950408889634
F32 = jnp.float32
BF16 = jnp.bfloat16
MESH = pl.DeviceIdType.MESH

ZW = 256
CW = (384, 384)
CO = (256, 640)
NC = len(CW)


def scratch():
    v, dma = pltpu.VMEM, pltpu.SemaphoreType.DMA
    s = {
        "q": v((256, 1024), BF16), "do": v((256, 1024), BF16),
        "w": v((4096, 256), BF16), "wt": v((256, 4096), BF16),
        "qt": v((8, 128, 256), BF16), "dot": v((8, 128, 256), BF16),
        "bias": v((4, 16, 256), F32),
        "part": v((512, 256), F32), "part_in": v((512, 256), F32),
        "kv": v((2, 512, 128), BF16), "kvt": v((2, 128, 512), BF16),
        "dkv": v((512, 256), BF16), "dkv_in": v((512, 256), BF16),
        "acc": v((2, 512, 128), F32),
        "gz": v((8, 2, 4, 2, 16, ZW), BF16), "pz": v((8, 2, 4, 2, 16, ZW), BF16),
        "rz1": v((2, 4, 2, 4, 2, 16, ZW), BF16), "rz2": v((16, 16, ZW), BF16),
    }
    for ch in range(NC):
        n = CW[ch]
        s |= {
            f"g{ch}": v((2, 8, 8, 16, n), BF16), f"pb{ch}": v((2, 8, 8, 16, n), BF16),
            f"r1o{ch}": v((2, 8, 16, n), BF16), f"r1n{ch}": v((2, 2, 8, 16, n), BF16),
            f"r1yo{ch}": v((2, 8, 16, n), BF16), f"r1yn{ch}": v((2, 4, 8, 16, n), BF16),
            f"sx{ch}": v((2, 8, 16, n), BF16), f"sy{ch}": v((4, 8, 16, n), BF16),
            f"r2x{ch}": v((4, 8, 16, n), BF16), f"r2y{ch}": v((4, 8, 16, n), BF16),
            f"tx{ch}": v((8, 16, n), BF16), f"ty{ch}": v((8, 16, n), BF16),
            f"r3{ch}": v((8, 16, n), BF16),
        }
    s |= {
        "lsem": dma((4,)),
        "ss1": dma((NC, 8)), "rs1": dma((NC, 2, 8)),
        "ss2": dma((NC, 2, 4)), "rs2x": dma((NC, 2)), "rs2y": dma((NC, 4)),
        "ss3": dma((NC, 2, 2, 3)), "rs3x": dma((NC, 2, 3)), "rs3y": dma((NC, 2, 2)),
        "ss4": dma((2,)), "rs4": dma((2,)),
        "ssr1": dma((NC, 2, 6)), "rsr1x": dma((NC, 3, 2)), "rsr1y": dma((NC, 5)),
        "ssr2": dma((NC, 2, 4)), "rsr2x": dma((NC, 4)), "rsr2y": dma((NC, 4)),
        "ssr3": dma((NC, 2, 8)), "rsr3": dma((NC, 8)),
        "ssz1": dma((4, 4)), "rsz1": dma((2, 4, 2)),
        "ssz3": dma((2, 4)), "rsz3": dma((2, 4)),
        "ssrz1": dma((2, 4)), "rsrz1": dma((2, 4)),
        "ssrz2": dma((16,)), "rsrz2": dma((16,)),
    }
    return s


NAMES = tuple(scratch())


def mm(a, b):
    return jnp.dot(a, b, preferred_element_type=F32)


def kernel(vis, wk, wv, q_in, do_in, lim, att_o, dq_o, gv_o, *rest):
    R = dict(zip(NAMES, rest, strict=True))
    q, do, w, wt = R["q"], R["do"], R["w"], R["wt"]
    gz, pz = R["gz"], R["pz"]
    G = [R[f"g{ch}"] for ch in range(NC)]
    PB = [R[f"pb{ch}"] for ch in range(NC)]

    seg, ten = lax.axis_index("segment"), lax.axis_index("tensor")
    zh, x, c = lax.div(seg, 8), lax.rem(lax.div(seg, 2), 4), lax.rem(seg, 2)
    y, zl = lax.div(ten, 2), lax.rem(ten, 2)
    z = zh * 2 + zl
    zi = zl * 4 + zh
    h, yp = lax.div(y, 2), lax.rem(y, 2)
    role = lax.rem(y + 4 - 2 * c, 4)
    home = c == h

    def dev(xx, yy, zz, cc):
        return (lax.div(zz, 2) * 8 + xx * 2 + cc, yy * 2 + lax.rem(zz, 2))

    def zind(zz):
        return lax.rem(zz, 2) * 4 + lax.div(zz, 2)

    def xo(d):
        return lax.rem(x + d + 4, 4)

    def yo(d):
        return lax.rem(y + d + 4, 4)

    def zo(d):
        return lax.rem(z + d + 8, 8)

    partner = dev(x, y, z, 1 - c)

    def rdma(src, dst, ss, rs, to):
        return pltpu.make_async_remote_copy(
            src_ref=src, dst_ref=dst, send_sem=ss, recv_sem=rs, device_id=to, device_id_type=MESH
        )

    def arrived(dst, rs):
        rdma(dst, dst, R["ss4"].at[0], rs, partner).wait_recv()

    def begin(cp):
        cp.start()

    def sent(cp):
        cp.wait_send()

    lsem = R["lsem"]
    qcopies = [
        pltpu.make_async_copy(q_in.at[0], q, lsem.at[0]),
        pltpu.make_async_copy(do_in.at[0], do, lsem.at[1]),
    ]
    wcopies = [
        pltpu.make_async_copy(wk.at[0], w.at[:, pl.ds(0, HD)], lsem.at[2]),
        pltpu.make_async_copy(wv.at[0], w.at[:, pl.ds(HD, HD)], lsem.at[3]),
    ]
    for cp in qcopies + wcopies:
        cp.start()

    barrier = pltpu.get_barrier_semaphore()
    greet = [dev(x, y, zo(d), cc) for d in range(1, 8) for cc in (0, 1)]
    greet += [dev(xo(d), yo(e), z, cc) for d in range(4) for e in range(4) for cc in (0, 1) if (d, e) != (0, 0)]
    greet += [partner]
    for other in greet:
        pl.semaphore_signal(barrier, inc=1, device_id=other, device_id_type=MESH)
    pl.semaphore_wait(barrier, len(greet))

    mine = (1 - c) * (x * 2 + yp) + c * (yp * 4 + x)

    def g1(ch, d):
        src = vis.at[:, pl.ds(CO[ch], CW[ch])]
        return rdma(src, G[ch].at[c, mine, zi], R["ss1"].at[ch, d], R["rs1"].at[ch, c, zi], dev(x, y, zo(d), h))

    def g1_local(ch):
        return pltpu.make_async_copy(
            vis.at[:, pl.ds(CO[ch], CW[ch])], G[ch].at[c, mine, zi], R["rs1"].at[ch, c, zi]
        )

    def g1_all(ch, act):
        for d in (4, 3, 5, 2, 6, 1, 7):
            act(g1(ch, d))

        @pl.when(c == 1 - h)
        def _():
            act(g1(ch, 0))

    def g1_own(ch):
        @pl.when(home)
        def _():
            g1_local(ch).start()

    def z1(d, e):
        return rdma(
            vis.at[:, pl.ds(0, ZW)], gz.at[zi, yp, x, c], R["ssz1"].at[d, e], R["rsz1"].at[yp, x, c],
            dev(xo(d), yo(e), z, h),
        )

    def z1_all(act):
        for d, e in ((2, 2), (2, 1), (2, 3), (1, 2), (3, 2), (1, 1), (1, 3), (3, 1), (3, 3), (2, 0), (0, 2), (1, 0), (3, 0), (0, 1), (0, 3)):
            act(z1(d, e))

        @pl.when(c == 1 - h)
        def _():
            act(z1(0, 0))

    g1_all(0, begin)
    g1_own(0)
    z1_all(begin)

    @pl.when(home)
    def _():
        pltpu.make_async_copy(vis.at[:, pl.ds(0, ZW)], gz.at[zi, yp, x, c], R["rsz1"].at[yp, x, c]).start()

    for ch in range(1, NC):
        g1_all(ch, begin)
        g1_own(ch)

    for cp in qcopies:
        cp.wait()
    qt, dot_, bias = R["qt"], R["dot"], R["bias"]

    @pl.loop(0, 8)
    def _(n):
        lanes = pl.ds(pl.multiple_of(n * HD, HD), HD)
        qt[n] = q[:, lanes].astype(F32).T.astype(BF16)
        dot_[n] = do[:, lanes].astype(F32).T.astype(BF16)

    def g2x(ch, d):
        blk = G[ch].at[0, x * 2 + yp]
        return rdma(blk, blk, R["ss2"].at[ch, 0, d], R["rs2x"].at[ch, yp], dev(x, yo(d), z, c))

    def g2y(ch, d):
        blk = G[ch].at[1, yp * 4 + x]
        return rdma(blk, blk, R["ss2"].at[ch, 1, d], R["rs2y"].at[ch, x], dev(xo(d), y, z, c))

    def step2(ch):
        @pl.when(home)
        def _():
            for zz in range(8):
                arrived(G[ch].at[0, x * 2 + yp, zz], R["rs1"].at[ch, 0, zz])
            for d in (2, 1, 3):
                g2x(ch, d).start()
            for zz in range(8):
                arrived(G[ch].at[1, yp * 4 + x, zz], R["rs1"].at[ch, 1, zz])
            for d in (2, 1, 3):
                g2y(ch, d).start()

    def z3(d, s):
        side = 1 - 2 * d
        if s < 3:
            blk = gz.at[zind(zo(-side * s))]
        else:
            blk = gz.at[zind(zo(-side * s)), d]
        return rdma(blk, blk, R["ssz3"].at[d, s], R["rsz3"].at[d, s], dev(x, y, zo(side), c))

    def z3_arrived(d, s):
        at = zind(zo(-(1 - 2 * d) * (s + 1)))
        arrived(gz.at[at] if s < 3 else gz.at[at, d], R["rsz3"].at[d, s])

    def zstep(s):
        for d in range(2):
            if s > 0:
                z3_arrived(d, s - 1)
            z3(d, s).start()

    def g3x(ch, d, half):
        blk = G[ch].at[0, x * 2 + half]
        return rdma(blk, blk, R["ss3"].at[ch, 0, d, half], R["rs3x"].at[ch, d, half], dev(xo(1 - 2 * d), y, z, c))

    def g3xf(ch, d):
        blk = G[ch].at[0, xo(2 * d - 1) * 2 + d]
        return rdma(blk, blk, R["ss3"].at[ch, 0, d, 2], R["rs3x"].at[ch, d, 2], dev(xo(1 - 2 * d), y, z, c))

    def half_y(k, j):
        return pl.ds(k * 4 + j * 2, 2)

    def g3y(ch, k, j, d):
        blk = G[ch].at[1, half_y(k, j)]
        return rdma(blk, blk, R["ss3"].at[ch, 1, d, j], R["rs3y"].at[ch, k, j], dev(x, yo(1 - 2 * d), z, c))

    def g3y_role(ch, r):
        order = ((0, 0, 0), (0, 1, 1), (0, 1, 0), (0, 0, 1)) if r == 0 else ((1, 0, 1), (1, 1, 0), (1, 1, 1), (1, 0, 0))
        return [g3y(ch, k, j, d) for k, j, d in order]

    passed = ((1, 0, 1), (0, 0, 0), (1, 1, 0), (0, 1, 1))

    def g3yf(ch, r):
        k, j, d = passed[r]
        blk = G[ch].at[1, half_y(k, j)]
        return rdma(blk, blk, R["ss3"].at[ch, 1, d, 2], R["rs3y"].at[ch, k, j], dev(x, yo(1 - 2 * d), z, c))

    def step3(ch):
        for k in range(2):
            @pl.when(role != k)
            def _():
                arrived(G[ch].at[0, x * 2 + k], R["rs2x"].at[ch, k])
        for d, half in ((0, 0), (1, 1), (0, 1), (1, 0)):
            g3x(ch, d, half).start()
        for r in (0, 1):
            @pl.when(role == r)
            def _():
                for d in range(1, 4):
                    arrived(G[ch].at[1, r * 4 + xo(d)], R["rs2y"].at[ch, xo(d)])
                for cp in g3y_role(ch, r):
                    cp.start()

    def forward3(ch):
        for d in range(2):
            arrived(G[ch].at[0, xo(2 * d - 1) * 2 + d], R["rs3x"].at[ch, d, d])
            g3xf(ch, d).start()
        for r in range(4):
            @pl.when(role == r)
            def _():
                k, j, _d = passed[r]
                arrived(G[ch].at[1, half_y(k, j)], R["rs3y"].at[ch, k, j])
                g3yf(ch, r).start()

    def rest3(ch):
        for d in range(2):
            arrived(G[ch].at[0, xo(2 * d - 1) * 2 + 1 - d], R["rs3x"].at[ch, d, 1 - d])
        for d in range(2):
            arrived(G[ch].at[0, xo(2) * 2 + d], R["rs3x"].at[ch, d, 2])
        for r in range(4):
            @pl.when(role == r)
            def _():
                for k in (0, 1):
                    if r == k:
                        continue
                    for j in (0, 1):
                        if (k, j) != passed[r][:2]:
                            arrived(G[ch].at[1, half_y(k, j)], R["rs3y"].at[ch, k, j])

    part, part_in = R["part"], R["part_in"]

    def project(ch):
        for p in range(2):
            rows = slice(p * 256, (p + 1) * 256)
            total = part[rows, :] if ch != 0 else jnp.zeros((256, 256), F32)
            for k in range(2):
                for l in range(2):
                    if p == 0:
                        a = jnp.concatenate(
                            [G[ch][0, xx * 2 + k, l * 4 : l * 4 + 4].reshape(64, CW[ch]) for xx in range(4)], axis=0
                        )
                    else:
                        a = G[ch][1, k * 4 : k * 4 + 4, l * 4 : l * 4 + 4].reshape(256, CW[ch])
                    base = (k * 2 + l) * 1024 + CO[ch]
                    total += mm(a, w[base : base + CW[ch], :])
            part[rows, :] = total

    def project_z():
        for p in range(2):
            rows = slice(p * 256, (p + 1) * 256)
            total = part[rows, :]
            for k in range(2):
                for l in range(2):
                    a = jnp.concatenate(
                        [gz[l * 4 : l * 4 + 4, k, xx, p].reshape(64, ZW) for xx in range(4)], axis=0
                    )
                    base = (k * 2 + l) * 1024
                    total += mm(a, w[base : base + ZW, :])
            part[rows, :] = total

    step2(0)
    for k in range(2):
        for xx in range(4):
            for cc in range(2):
                arrived(gz.at[zi, k, xx, cc], R["rsz1"].at[k, xx, cc])
    zstep(0)
    for ch in range(1, NC):
        step2(ch)

    for cp in wcopies:
        cp.wait()

    @pl.loop(0, 8)
    def _(n):
        rows = pl.ds(pl.multiple_of(n * 256, 256), 256)
        wt[:, rows] = w[rows, :].astype(F32).T.astype(BF16)

    step3(0)
    zstep(1)

    @pl.loop(8, 16)
    def _(n):
        rows = pl.ds(pl.multiple_of(n * 256, 256), 256)
        wt[:, rows] = w[rows, :].astype(F32).T.astype(BF16)

    for ch in range(1, NC):
        step3(ch)
    limit = (1 - c) * lim[0:1, :] + c * lim[1:2, :]
    for t in range(4):
        bias[t] = jnp.broadcast_to(jnp.where(t < limit, 0.0, -1e30), (16, 256))
    forward3(0)
    zstep(2)
    for ch in range(1, NC):
        forward3(ch)
    rest3(0)
    project(0)
    zstep(3)
    for d in range(2):
        z3_arrived(d, 3)
    project_z()
    for ch in range(1, NC):
        rest3(ch)
        project(ch)

    swap = rdma(part, part_in, R["ss4"].at[0], R["rs4"].at[0], partner)
    swap.start()
    swap.wait()
    kv, kvt, acc = R["kv"], R["kvt"], R["acc"]
    pre = part[...] + part_in[...]
    part[...] = pre
    kp = pre[:, :HD]
    inv = lax.rsqrt(jnp.mean(kp * kp, axis=-1, keepdims=True) + EPS)
    keys = (kp * inv).astype(BF16)
    vals = pre[:, HD:].astype(BF16)
    kv[0] = keys
    kv[1] = vals
    kvt[0] = keys.astype(F32).T.astype(BF16)
    kvt[1] = vals.astype(F32).T.astype(BF16)

    acc[...] = jnp.zeros_like(acc)

    @pl.loop(0, 8, unroll=2)
    def _(n):
        lanes = pl.ds(pl.multiple_of(n * HD, HD), HD)
        qn = q[:, lanes]
        don = do[:, lanes]
        dotn = dot_[n]
        s = mm(kv[0], qt[n]) * (SCALE * LOG2E)
        s = (s.reshape(8, 4, 16, 256) + bias[...][None]).reshape(512, 256)
        m = jnp.max(s, axis=0, keepdims=True)
        e = jnp.exp2(s - m)
        prob = e * (1.0 / jnp.sum(e, axis=0, keepdims=True))
        pb16 = prob.astype(BF16)
        at = mm(kvt[1], pb16).astype(BF16).astype(F32)
        dp = mm(kv[1], dotn)
        delta = jnp.sum(at * dotn.astype(F32), axis=0, keepdims=True)
        ds = (prob * (dp - delta)).astype(BF16)
        att_o[0, :, lanes] = at.T.astype(BF16)
        dqt = mm(kvt[0], ds) * SCALE
        dq_o[0, :, lanes] = dqt.T.astype(BF16)
        acc[0] += mm(ds, qn)
        acc[1] += mm(pb16, don)

    dkv, dkv_in = R["dkv"], R["dkv_in"]
    kp = part[:, :HD]
    inv = lax.rsqrt(jnp.mean(kp * kp, axis=-1, keepdims=True) + EPS)
    dk = acc[0] * SCALE
    dkp = inv * dk - kp * (inv * inv * inv * jnp.mean(kp * dk, axis=-1, keepdims=True))
    dkv[:, :HD] = dkp.astype(BF16)
    dkv[:, HD:] = acc[1].astype(BF16)
    swap2 = rdma(dkv, dkv_in, R["ss4"].at[1], R["rs4"].at[1], partner)
    swap2.start()
    swap2.wait()

    def back(p, base, n):
        rows = slice(p * 256, (p + 1) * 256)
        wtb = wt[:, base : base + n]
        return (mm(dkv[rows, :], wtb) + mm(dkv_in[rows, :], wtb)).astype(BF16)

    def back_z():
        for k in range(2):
            for l in range(2):
                for p in range(2):
                    v = back(p, (k * 2 + l) * 1024, ZW)
                    for xx in range(4):
                        pz[l * 4 : l * 4 + 4, k, xx, p] = v[xx * 64 : (xx + 1) * 64].reshape(4, 16, ZW)

    def back_chunk(ch):
        pb = PB[ch]
        for k in range(2):
            for l in range(2):
                for p in range(2):
                    v = back(p, (k * 2 + l) * 1024 + CO[ch], CW[ch])
                    if p == 0:
                        for xx in range(4):
                            pb[0, xx * 2 + k, l * 4 : l * 4 + 4] = v[xx * 64 : (xx + 1) * 64].reshape(4, 16, CW[ch])
                    else:
                        pb[1, k * 4 : k * 4 + 4, l * 4 : l * 4 + 4] = v.reshape(4, 4, 16, CW[ch])

    rz1, rz2 = R["rz1"], R["rz2"]

    def rz(d, s):
        side = 1 - 2 * d
        at = zind(zo(side * (4 - s)))
        src = pz.at[at, d] if s == 0 else pz.at[at]
        dst = rz1.at[d, 0, d] if s == 0 else rz1.at[d, s]
        return rdma(src, dst, R["ssrz1"].at[d, s], R["rsrz1"].at[d, s], dev(x, y, zo(side), c))

    def rz_arrived(d, s):
        arrived(rz1.at[d, 0, d] if s == 0 else rz1.at[d, s], R["rsrz1"].at[d, s])

    def rzstep(s):
        for d in range(2):
            if s > 0:
                rz_arrived(d, s - 1)
                at = zind(zo((1 - 2 * d) * (4 - s)))
                if s == 1:
                    pz[at, d] = (pz[at, d].astype(F32) + rz1[d, 0, d].astype(F32)).astype(BF16)
                else:
                    pz[at] = (pz[at].astype(F32) + rz1[d, s - 1].astype(F32)).astype(BF16)
            rz(d, s).start()

    def rz2_to(k, xx, cc):
        i = (yp * 4 + x) * 2 + cc
        return i

    def z2(d, k, cc):
        src = pz.at[zi, k, xo(d), cc]
        me = y * 4 + x
        return rdma(src, rz2.at[me], R["ssrz2"].at[(k * 4 + d) * 2 + cc], R["rsrz2"].at[me], dev(xo(d), 2 * c + k, z, cc))

    def z2_all(act):
        for d in (2, 1, 3):
            for k in range(2):
                for cc in range(2):
                    act(z2(d, k, cc))
        for k in range(2):
            for cc in range(2):
                if True:
                    @pl.when(jnp.logical_or(role != k, c != cc))
                    def _():
                        act(z2(0, k, cc))

    def z2_local():
        return pltpu.make_async_copy(pz.at[zi, yp, x, c], rz2.at[y * 4 + x], R["rsrz2"].at[y * 4 + x])

    def rz_sum():
        for d in range(2):
            rz_arrived(d, 3)
        pz[zi] = (pz[zi].astype(F32) + rz1[0, 3].astype(F32) + rz1[1, 3].astype(F32)).astype(BF16)
        z2_all(begin)

        @pl.when(home)
        def _():
            z2_local().start()

    def r1x_opp(ch, d):
        return rdma(
            PB[ch].at[0, xo(2) * 2 + d], R[f"r1o{ch}"].at[d], R["ssr1"].at[ch, 0, d], R["rsr1x"].at[ch, 0, d],
            dev(xo(1 - 2 * d), y, z, c),
        )

    def r1x_free(ch, d):
        return rdma(
            PB[ch].at[0, xo(1 - 2 * d) * 2 + 1 - d], R[f"r1n{ch}"].at[d, 1 - d], R["ssr1"].at[ch, 0, 2 + d],
            R["rsr1x"].at[ch, 1, d], dev(xo(1 - 2 * d), y, z, c),
        )

    def r1x_dep(ch, d):
        return rdma(
            PB[ch].at[0, xo(1 - 2 * d) * 2 + d], R[f"r1n{ch}"].at[d, d], R["ssr1"].at[ch, 0, 4 + d],
            R["rsr1x"].at[ch, 2, d], dev(xo(1 - 2 * d), y, z, c),
        )

    y_opp = {2: ((1, 0, 0), (0, 0, 1)), 3: ((0, 1, 0), (1, 1, 1))}
    y_free = {0: (0, 1, 1), 1: (1, 0, 1), 2: (1, 1, 0), 3: (0, 0, 0)}
    y_dep = {0: (0, 1, 0), 1: (1, 0, 0), 2: (1, 1, 1), 3: (0, 0, 1)}

    def r1y_opp(ch, r, i):
        d, k, j = y_opp[r][i]
        return rdma(
            PB[ch].at[1, half_y(k, j)], R[f"r1yo{ch}"], R["ssr1"].at[ch, 1, i], R["rsr1y"].at[ch, 0],
            dev(x, yo(1 - 2 * d), z, c),
        )

    def r1y_next(ch, r, dep):
        d, k, j = (y_dep if dep else y_free)[r]
        side = 0 if r >= 2 else 1
        return rdma(
            PB[ch].at[1, half_y(k, j)], R[f"r1yn{ch}"].at[side, pl.ds(j * 2, 2)], R["ssr1"].at[ch, 1, 2 + dep],
            R["rsr1y"].at[ch, 1 + dep + side * 2], dev(x, yo(1 - 2 * d), z, c),
        )

    def rs1(ch):
        for d in range(2):
            r1x_opp(ch, d).start()
        for r in (2, 3):
            @pl.when(role == r)
            def _():
                for i in range(2):
                    r1y_opp(ch, r, i).start()
        for d in range(2):
            r1x_free(ch, d).start()
        for r in range(4):
            @pl.when(role == r)
            def _():
                r1y_next(ch, r, 0).start()

    def rs1_dep(ch):
        pb, r1o, r1yo = PB[ch], R[f"r1o{ch}"], R[f"r1yo{ch}"]
        for d in range(2):
            arrived(r1o.at[d], R["rsr1x"].at[ch, 0, d])
            to = xo(1 - 2 * d) * 2 + d

            @pl.loop(0, 8, unroll=2)
            def _(i):
                pb[0, to, i] = (pb[0, to, i].astype(F32) + r1o[d, i].astype(F32)).astype(BF16)

            r1x_dep(ch, d).start()
        arrived(r1yo, R["rsr1y"].at[ch, 0])
        for r in range(4):
            @pl.when(role == r)
            def _():
                _d, k, j = y_dep[r]

                @pl.loop(0, 8)
                def _(i):
                    for xx in range(2):
                        at = k * 4 + j * 2 + xx
                        pb[1, at, i] = (pb[1, at, i].astype(F32) + r1yo[xx, i].astype(F32)).astype(BF16)

                r1y_next(ch, r, 1).start()

    def r2x_to(ch, k):
        return rdma(
            R[f"sx{ch}"].at[k], R[f"r2x{ch}"].at[y], R["ssr2"].at[ch, 0, k], R["rsr2x"].at[ch, y],
            dev(x, 2 * c + k, z, c),
        )

    def r2y_to(ch, d):
        return rdma(
            R[f"sy{ch}"].at[xo(d)], R[f"r2y{ch}"].at[x], R["ssr2"].at[ch, 1, d], R["rsr2y"].at[ch, x],
            dev(xo(d), y, z, c),
        )

    def rs2(ch):
        pb, r1n, r1yn, sx, sy = PB[ch], R[f"r1n{ch}"], R[f"r1yn{ch}"], R[f"sx{ch}"], R[f"sy{ch}"]
        for d in range(2):
            arrived(r1n.at[d, 1 - d], R["rsr1x"].at[ch, 1, d])
        for d in range(2):
            arrived(r1n.at[d, d], R["rsr1x"].at[ch, 2, d])

        @pl.loop(0, 8)
        def _(b):
            for k in range(2):
                sx[k, b] = (
                    pb[0, x * 2 + k, b].astype(F32) + r1n[0, k, b].astype(F32) + r1n[1, k, b].astype(F32)
                ).astype(BF16)

        for k in range(2):
            @pl.when(role != k)
            def _():
                r2x_to(ch, k).start()

        @pl.when(home)
        def _():
            arrived(r1yn.at[0, pl.ds(0, 2)], R["rsr1y"].at[ch, 1])
            arrived(r1yn.at[1, pl.ds(2, 2)], R["rsr1y"].at[ch, 3])
            arrived(r1yn.at[0, pl.ds(2, 2)], R["rsr1y"].at[ch, 2])
            arrived(r1yn.at[1, pl.ds(0, 2)], R["rsr1y"].at[ch, 4])

            @pl.loop(0, 8)
            def _(b):
                for k in range(4):
                    sy[k, b] = (
                        pb[1, yp * 4 + k, b].astype(F32) + r1yn[0, k, b].astype(F32) + r1yn[1, k, b].astype(F32)
                    ).astype(BF16)

            for d in (2, 1, 3):
                r2y_to(ch, d).start()

    def r3_to(ch, cc, d):
        t = R[f"ty{ch}" if cc else f"tx{ch}"]
        zz = zo(d)
        return rdma(t.at[zind(zz)], R[f"r3{ch}"].at[zi], R["ssr3"].at[ch, cc, d], R["rsr3"].at[ch, zi], dev(x, y, zz, cc))

    def r3_all(ch, cc, act):
        for d in (4, 3, 5, 2, 6, 1, 7):
            act(r3_to(ch, cc, d))

        @pl.when(c != cc)
        def _():
            act(r3_to(ch, cc, 0))

    def r3_own(ch, cc):
        t = R[f"ty{ch}" if cc else f"tx{ch}"]

        @pl.when(c == cc)
        def _():
            pltpu.make_async_copy(t.at[zi], R[f"r3{ch}"].at[zi], R["rsr3"].at[ch, zi]).start()

    def rs3(ch):
        sx, sy, r2x, r2y, tx, ty = (R[f"{n}{ch}"] for n in ("sx", "sy", "r2x", "r2y", "tx", "ty"))

        @pl.when(home)
        def _():
            for d in range(1, 4):
                arrived(r2x.at[yo(d)], R["rsr2x"].at[ch, yo(d)])

            @pl.loop(0, 8, unroll=2)
            def _(b):
                v = sx[yp, b].astype(F32)
                for d in range(1, 4):
                    v += r2x[yo(d), b].astype(F32)
                tx[b] = v.astype(BF16)

            r3_all(ch, 0, begin)
            r3_own(ch, 0)
            for d in range(1, 4):
                arrived(r2y.at[xo(d)], R["rsr2y"].at[ch, xo(d)])

            @pl.loop(0, 8, unroll=2)
            def _(b):
                v = sy[x, b].astype(F32)
                for d in range(1, 4):
                    v += r2y[xo(d), b].astype(F32)
                ty[b] = v.astype(BF16)

            r3_all(ch, 1, begin)
            r3_own(ch, 1)

    def finish(ch):
        r3 = R[f"r3{ch}"]
        for b in range(8):
            arrived(r3.at[b], R["rsr3"].at[ch, b])
        total = r3[0].astype(F32)
        for b in range(1, 8):
            total += r3[b].astype(F32)
        gv_o[:, CO[ch] : CO[ch] + CW[ch]] = total

    back_z()
    rzstep(0)
    for ch in range(NC):
        back_chunk(ch)
        rs1(ch)
    rs1_dep(0)
    rzstep(1)
    for ch in range(1, NC):
        rs1_dep(ch)
    rs2(0)
    rzstep(2)
    for ch in range(1, NC):
        rs2(ch)
    rs3(0)
    rzstep(3)
    for ch in range(1, NC):
        rs3(ch)
    rz_sum()
    for ch in range(NC):
        finish(ch)
    for i in range(16):
        arrived(rz2.at[i], R["rsrz2"].at[i])
    total = rz2[0].astype(F32)
    for i in range(1, 16):
        total += rz2[i].astype(F32)
    gv_o[:, :ZW] = total

    z1_all(sent)
    z2_all(sent)
    for d in range(2):
        for s in range(4):
            sent(z3(d, s))
            sent(rz(d, s))
    for ch in range(NC):
        g1_all(ch, sent)

        @pl.when(home)
        def _():
            for d in range(1, 4):
                sent(g2x(ch, d))
                sent(g2y(ch, d))
                sent(r2y_to(ch, d))
            for cc in range(2):
                r3_all(ch, cc, sent)

        for d in range(2):
            for half in range(2):
                sent(g3x(ch, d, half))
            sent(g3xf(ch, d))
            sent(r1x_opp(ch, d))
            sent(r1x_free(ch, d))
            sent(r1x_dep(ch, d))
        for r in range(4):
            @pl.when(role == r)
            def _():
                if r < 2:
                    for cp in g3y_role(ch, r):
                        sent(cp)
                else:
                    for i in range(2):
                        sent(r1y_opp(ch, r, i))
                sent(g3yf(ch, r))
                sent(r1y_next(ch, r, 0))
                sent(r1y_next(ch, r, 1))
        for k in range(2):
            @pl.when(role != k)
            def _():
                sent(r2x_to(ch, k))


def on_device(queries, grad_attended, vision, key_weight, value_weight, tile_limit):
    vmem = pl.BlockSpec(memory_space=pltpu.VMEM)
    hbm = pl.BlockSpec(memory_space=pl.ANY)
    return pl.pallas_call(
        kernel,
        out_shape=(
            jax.ShapeDtypeStruct(queries.shape, BF16),
            jax.ShapeDtypeStruct(queries.shape, BF16),
            jax.ShapeDtypeStruct(vision.shape, F32),
        ),
        in_specs=[hbm, hbm, hbm, hbm, hbm, vmem],
        out_specs=(vmem, vmem, vmem),
        scratch_shapes=list(scratch().values()),
        compiler_params=pltpu.CompilerParams(
            collective_id=0, has_side_effects=True, vmem_limit_bytes=56 * 2**20
        ),
        cost_estimate=pl.CostEstimate(flops=6_000_000_000, bytes_accessed=6_000_000, transcendentals=1_000_000),
    )(vision, key_weight, value_weight, queries, grad_attended, tile_limit.reshape(2, 256))


def solution(mesh):
    return jax.shard_map(
        on_device,
        mesh=mesh,
        in_specs=(
            P("segment", None, "tensor"),
            P("segment", None, "tensor"),
            P("segment", "tensor"),
            P("segment", None, "tensor"),
            P("segment", None, "tensor"),
            P(),
        ),
        out_specs=(
            P("segment", None, "tensor"),
            P("segment", None, "tensor"),
            P("segment", "tensor"),
        ),
        check_vma=False,
    )
```

time: 321 us -> 94.5 us (0.29); the launches traced: 317 us -> 94.2 us
  waiting for transfers between devices: 215 us -> 0 us
  Pallas kernels: 0 us -> 88.9 us
  matrix products: 32 us -> 0 us
  blocking collectives: 26.7 us -> 0 us
  between operations: 13.9 us -> 0.65 us
  other arithmetic: 12.6 us -> 0 us
  starting transfers between devices: 8.02 us -> 0 us
  local copies, waits for them, and re-layouts: 8.76 us -> 4.69 us
    reduce_scatter x2 -> x0, waiting for transfers between devices: 155 us -> none  [the longest x1 121 us: on_device(): lax.psum_scatter((term + jnp.dot(grad_vals, value_matrix.T, preferred_ele...]
    pallas_call x0 -> x1, Pallas kernels: none -> 88.9 us  [on_device(): pl.pallas_call(kernel, out_shape=(jax.ShapeDtypeStruct(queries.shape, BF1...]
    all_gather x1 -> x0, waiting for transfers between devices: 59.6 us -> none  [on_device(): lax.all_gather(widened, 'segment', axis=0, tiled=True)]
    dot_general x8 -> x0, matrix products: 32 us -> none  [the longest x1 11.6 us: on_device(): jnp.dot(grad_vals, value_matrix.T, preferred_element_type=jnp.float32)]
    all_gather x1 -> x0, blocking collectives: 26.7 us -> none  [on_device(): widened = lax.all_gather(vision, 'tensor', axis=1, tiled=True)]
    squeeze x1 -> x0, other arithmetic: 8.28 us -> none  [on_device(): key_matrix = full_weights[0]]
    ppermute x1 -> x0, starting transfers between devices: 7.89 us -> none  [from_partner(): return lax.ppermute(value, axis, pairs)]
  transfers between devices with their start and end apart: 4 -> 0, of which waited for: 4 -> 0; matrix products, arithmetic and copies ran while one was open for 6% -> 0% of each run, Pallas kernels for 0% -> 0%
where the time goes in v2:
time: 94.5 us; the launch traced here: 94.2 us
  Pallas kernels  88.9 us (94%)
  local copies, waits for them, and re-layouts  4.69 us (5%)
    pallas_call x1, Pallas kernels, on_device(): pl.pallas_call(kernel, out_shape=(jax.ShapeDtypeStruct(queries.shape, BF1...  88.9 us
    unnamed x7, local copies, waits for them, and re-layouts  3.42 us

profile of v2, /device:TPU:1, one launch (start us, length us, event | category | flops | bytes accessed | tf_op | source)
XLA Modules:
  0.0 94.2 jit_solution(956455806241762434)
XLA Ops:
  0.6 1.3 %reshape.9.lim = s32[2,256]{1,0:T(2,128)} reshape(s32[512]{0:T(512)} %param.11) | data formatting | bytes 4096 | tf_op jit(solution)/shard_map/reshape | solution.py:781
  1.9 88.9 %shard_map.85 = (bf16[1,256,1024]{2,1,0:T(8,128)(2,1)}, bf16[1,256,1024]{2,1,0:T(8,128)(2,1)}, f32[16,1024]{1,0:T(8,128)}) custom-call(bf16[16,1024]{1,0:T(8,128)(2,1)} %vis.1, bf16[1,4096,128]{2,1,0:T(8,128)(2,1)} %wk.1, bf16[1,4096,128]{2,1,0:T(8,128)(2,1)} %wv.1, bf16[1,256,1024]{2,1,0:T(8,128)(2,1)} %q_in.1, bf16[1,256,1024]{2,1,0:T(8,128)(2,1)} %do_in.1, ...), custom_call_target="tpu_custom_call" | custom-call | flops 6000000000 | bytes 6000000 | tf_op jit(solution)/shard_map/pallas_call | solution.py:767
  90.8 0.0 copy-start
  90.8 1.9 %copy.12 = bf16[1,256,1024]{2,1,0:T(8,128)(2,1)} copy(bf16[1,256,1024]{2,1,0:T(8,128)(2,1)} %get-tuple-element.6) | data formatting | bytes 1048576
  92.7 0.0 copy-done
  92.7 0.0 copy-start.1
  92.7 0.8 copy.13
  93.5 0.1 copy-done.1
  93.6 0.6 copy.14
Async XLA Ops:
  90.8 1.9 %copy-start = (bf16[1,256,1024]{2,1,0:T(8,128)(2,1)S(1)}, bf16[1,256,1024]{2,1,0:T(8,128)(2,1)}, u32[]{:S(2)}) copy-start(bf16[1,256,1024]{2,1,0:T(8,128)(2,1)} %get-tuple-element.7) | copy-start | bytes 1572868
  92.7 0.9 copy-start.1

commit v3 on v0

v3 whole, which is shorter than its diff:
```python
import jax
import jax.numpy as jnp
from jax import lax
from jax.experimental import pallas as pl
from jax.experimental.pallas import tpu as pltpu
from jax.sharding import PartitionSpec as P

HD = 128
EPS = 1e-05
SCALE = HD ** (-0.5)
LOG2E = 1.4426950408889634
F32 = jnp.float32
BF16 = jnp.bfloat16
MESH = pl.DeviceIdType.MESH

ZW, XW, YW = 256, 384, 384
XO, YO = ZW, ZW + XW


def scratch():
    v, dma = pltpu.VMEM, pltpu.SemaphoreType.DMA
    s = {
        "q": v((8, 256, 128), BF16), "do": v((8, 256, 128), BF16),
        "w": v((4096, 256), BF16), "wt": v((256, 4096), BF16),
        "qt": v((8, 128, 256), BF16), "dot": v((8, 128, 256), BF16),
        "bias": v((4, 16, 256), F32),
        "part": v((512, 256), F32), "part_in": v((512, 256), F32),
        "kv": v((2, 512, 128), BF16), "kvt": v((2, 128, 512), BF16),
        "probs": v((512, 2048), BF16), "dsc": v((512, 2048), BF16), "at": v((8, 128, 256), BF16),
        "dkv": v((512, 256), BF16), "dkv_in": v((512, 256), BF16),
        "att_v": v((256, 1024), BF16), "dq_v": v((256, 1024), BF16), "gv_v": v((16, 1024), F32),
        "gz": v((2, 8, 2, 4, 16, ZW), BF16), "pz": v((2, 8, 2, 4, 16, ZW), BF16),
        "rz1": v((2, 2, 4, 2, 4, 16, ZW), BF16), "rzy": v((2, 4, 4, 16, ZW), BF16),
        "tz": v((2, 4, 16, ZW), BF16), "rzx": v((4, 16, ZW), BF16),
        "gx": v((2, 8, 8, 16, XW), BF16), "gy": v((2, 8, 8, 16, YW), BF16),
        "px": v((2, 8, 8, 16, XW), BF16), "py": v((2, 8, 8, 16, YW), BF16),
        "r1o": v((2, 2, 8, 16, XW), BF16), "r1n": v((2, 2, 2, 8, 16, XW), BF16),
        "r1yo": v((2, 2, 8, 16, YW), BF16), "r1yn": v((2, 2, 4, 8, 16, YW), BF16),
        "sx": v((2, 2, 8, 16, XW), BF16), "sy": v((2, 4, 8, 16, YW), BF16),
        "r2x": v((2, 4, 8, 16, XW), BF16), "r2y": v((2, 4, 8, 16, YW), BF16),
        "tx": v((2, 8, 16, XW), BF16), "ty": v((2, 8, 16, YW), BF16),
        "r3x": v((8, 16, XW), BF16), "r3y": v((8, 16, YW), BF16),
        "lsem": dma((8,)), "osem": dma((3,)),
        "ss1": dma((2, 8)), "rs1": dma((2, 2, 8)),
        "ss2": dma((2, 2, 4)), "rs2x": dma((2, 2)), "rs2y": dma((2, 4)),
        "ss3": dma((2, 2, 2, 3)), "rs3x": dma((2, 2, 3)), "rs3y": dma((2, 2, 2)),
        "ss4": dma((4,)), "rs4": dma((4,)),
        "ssr1": dma((2, 2, 6)), "rsr1x": dma((2, 3, 2)), "rsr1y": dma((2, 5)),
        "ssr2": dma((2, 2, 4)), "rsr2x": dma((2, 4)), "rsr2y": dma((2, 4)),
        "ssr3": dma((2, 2, 8)), "rsr3": dma((2, 8)),
        "ssz1": dma((4,)), "rsz1": dma((2, 4)), "ssz2": dma((2, 4)), "rsz2": dma((2, 2)),
        "ssz3": dma((2, 2, 4)), "rsz3": dma((2, 2, 4)),
        "ssrz1": dma((2, 2, 4)), "rsrz1": dma((2, 2, 4)),
        "ssrz2": dma((2, 2)), "rsrz2": dma((2, 4)), "ssrz3": dma((2, 4)), "rsrz3": dma((4,)),
    }
    return s


NAMES = tuple(scratch())


def mm(a, b):
    return jnp.dot(a, b, preferred_element_type=F32)


def kernel(vis, wk, wv, q_in, do_in, lim, att_o, dq_o, gv_o, *rest):
    R = dict(zip(NAMES, rest, strict=True))
    q, do, w, wt = R["q"], R["do"], R["w"], R["wt"]
    gx, gy, gz, px, py, pz = (R[n] for n in ("gx", "gy", "gz", "px", "py", "pz"))

    seg, ten = lax.axis_index("segment"), lax.axis_index("tensor")
    zh, x, c = lax.div(seg, 8), lax.rem(lax.div(seg, 2), 4), lax.rem(seg, 2)
    y, zl = lax.div(ten, 2), lax.rem(ten, 2)
    z = zh * 2 + zl
    zi = zl * 4 + zh
    h, yp = lax.div(y, 2), lax.rem(y, 2)
    role = lax.rem(y + 4 - 2 * c, 4)
    home = c == h

    def dev(xx, yy, zz, cc):
        return (lax.div(zz, 2) * 8 + xx * 2 + cc, yy * 2 + lax.rem(zz, 2))

    def zind(zz):
        return lax.rem(zz, 2) * 4 + lax.div(zz, 2)

    def xo(d):
        return lax.rem(x + d + 4, 4)

    def yo(d):
        return lax.rem(y + d + 4, 4)

    def zo(d):
        return lax.rem(z + d + 8, 8)

    partner = dev(x, y, z, 1 - c)

    def rdma(src, dst, ss, rs, to):
        return pltpu.make_async_remote_copy(
            src_ref=src, dst_ref=dst, send_sem=ss, recv_sem=rs, device_id=to, device_id_type=MESH
        )

    def arrived(dst, rs):
        rdma(dst, dst, R["ss4"].at[0], rs, partner).wait_recv()

    def begin(cp):
        cp.start()

    def sent(cp):
        cp.wait_send()

    lsem = R["lsem"]
    wcopies = [
        pltpu.make_async_copy(wk.at[0], w.at[:, pl.ds(0, HD)], lsem.at[0]),
        pltpu.make_async_copy(wv.at[0], w.at[:, pl.ds(HD, HD)], lsem.at[1]),
    ]

    barrier = pltpu.get_barrier_semaphore()
    greet = [dev(x, y, zo(d), cc) for d in range(1, 8) for cc in (0, 1)]
    greet += [dev(xo(d), y, z, cc) for d in range(1, 4) for cc in (0, 1)]
    greet += [dev(x, yo(d), z, c) for d in range(1, 4)] + [partner]
    for other in greet:
        pl.semaphore_signal(barrier, inc=1, device_id=other, device_id_type=MESH)
    for cp in wcopies:
        cp.start()
    loads = [
        pltpu.make_async_copy(q_in.at[0], R["att_v"], lsem.at[2]),
        pltpu.make_async_copy(do_in.at[0], R["dq_v"], lsem.at[3]),
    ]
    for cp in loads:
        cp.start()
    pl.semaphore_wait(barrier, len(greet))

    def z1(d):
        return rdma(vis.at[:, pl.ds(0, ZW)], gz.at[c, zi, yp, x], R["ssz1"].at[d], R["rsz1"].at[c, x], dev(xo(d), y, z, h))

    def z1_all(act):
        for d in (2, 1, 3):
            act(z1(d))

        @pl.when(c == 1 - h)
        def _():
            act(z1(0))

    def g1(route, d):
        src, dst = (
            (vis.at[:, pl.ds(XO, XW)], gx.at[c, x * 2 + yp, zi]),
            (vis.at[:, pl.ds(YO, YW)], gy.at[c, yp * 4 + x, zi]),
        )[route]
        return rdma(src, dst, R["ss1"].at[route, d], R["rs1"].at[c, route, zi], dev(x, y, zo(d), h))

    def g1_all(route, act):
        for d in (4, 3, 5, 2, 6, 1, 7):
            act(g1(route, d))

        @pl.when(c == 1 - h)
        def _():
            act(g1(route, 0))

    z1_all(begin)
    for route in range(2):
        g1_all(route, begin)

    @pl.when(home)
    def _():
        pltpu.make_async_copy(vis.at[:, pl.ds(0, ZW)], gz.at[c, zi, yp, x], R["rsz1"].at[c, x]).start()
        pltpu.make_async_copy(vis.at[:, pl.ds(XO, XW)], gx.at[c, x * 2 + yp, zi], R["rs1"].at[c, 0, zi]).start()
        pltpu.make_async_copy(vis.at[:, pl.ds(YO, YW)], gy.at[c, yp * 4 + x, zi], R["rs1"].at[c, 1, zi]).start()

    for cp in loads:
        cp.wait()
    qt, dot_, bias = R["qt"], R["dot"], R["bias"]

    @pl.loop(0, 8)
    def _(n):
        lanes = pl.ds(pl.multiple_of(n * HD, HD), HD)
        qn = R["att_v"][:, lanes]
        dn = R["dq_v"][:, lanes]
        q[n] = qn
        do[n] = dn
        qt[n] = qn.astype(F32).T.astype(BF16)
        dot_[n] = dn.astype(F32).T.astype(BF16)

    def z2(r, d):
        blk = gz.at[r, zi, yp]
        return rdma(blk, blk, R["ssz2"].at[r, d], R["rsz2"].at[r, yp], dev(x, yo(d), z, c))

    @pl.when(home)
    def _():
        for r in range(2):
            for xx in range(4):
                arrived(gz.at[r, zi, yp, xx], R["rsz1"].at[r, xx])
            for d in (2, 1, 3):
                z2(r, d).start()

    def g2x(r, d):
        blk = gx.at[r, x * 2 + yp]
        return rdma(blk, blk, R["ss2"].at[r, 0, d], R["rs2x"].at[r, yp], dev(x, yo(d), z, c))

    def g2y(r, d):
        blk = gy.at[r, yp * 4 + x]
        return rdma(blk, blk, R["ss2"].at[r, 1, d], R["rs2y"].at[r, x], dev(xo(d), y, z, c))

    def step2(r):
        @pl.when(home)
        def _():
            for zz in range(8):
                arrived(gx.at[r, x * 2 + yp, zz], R["rs1"].at[r, 0, zz])
            for d in (2, 1, 3):
                g2x(r, d).start()
            for zz in range(8):
                arrived(gy.at[r, yp * 4 + x, zz], R["rs1"].at[r, 1, zz])
            for d in (2, 1, 3):
                g2y(r, d).start()

    def z3(r, d, s):
        side = 1 - 2 * d
        at = zind(zo(-side * s))
        blk = gz.at[r, at] if s < 3 else gz.at[r, at, d]
        return rdma(blk, blk, R["ssz3"].at[r, d, s], R["rsz3"].at[r, d, s], dev(x, y, zo(side), c))

    def z3_arrived(r, d, s):
        at = zind(zo(-(1 - 2 * d) * (s + 1)))
        arrived(gz.at[r, at] if s < 3 else gz.at[r, at, d], R["rsz3"].at[r, d, s])

    def zstep(r, s):
        if s == 0:
            for k in range(2):
                @pl.when(role != k)
                def _():
                    arrived(gz.at[r, zi, k], R["rsz2"].at[r, k])
        for d in range(2):
            if s > 0:
                z3_arrived(r, d, s - 1)
            z3(r, d, s).start()

    def g3x(r, d, half):
        blk = gx.at[r, x * 2 + half]
        return rdma(blk, blk, R["ss3"].at[r, 0, d, half], R["rs3x"].at[r, d, half], dev(xo(1 - 2 * d), y, z, c))

    def g3xf(r, d):
        blk = gx.at[r, xo(2 * d - 1) * 2 + d]
        return rdma(blk, blk, R["ss3"].at[r, 0, d, 2], R["rs3x"].at[r, d, 2], dev(xo(1 - 2 * d), y, z, c))

    def half_y(k, j):
        return pl.ds(k * 4 + j * 2, 2)

    def g3y(r, k, j, d):
        blk = gy.at[r, half_y(k, j)]
        return rdma(blk, blk, R["ss3"].at[r, 1, d, j], R["rs3y"].at[r, k, j], dev(x, yo(1 - 2 * d), z, c))

    def g3y_role(r, o):
        order = ((0, 0, 0), (0, 1, 1), (0, 1, 0), (0, 0, 1)) if o == 0 else ((1, 0, 1), (1, 1, 0), (1, 1, 1), (1, 0, 0))
        return [g3y(r, k, j, d) for k, j, d in order]

    passed = ((1, 0, 1), (0, 0, 0), (1, 1, 0), (0, 1, 1))

    def g3yf(r, o):
        k, j, d = passed[o]
        blk = gy.at[r, half_y(k, j)]
        return rdma(blk, blk, R["ss3"].at[r, 1, d, 2], R["rs3y"].at[r, k, j], dev(x, yo(1 - 2 * d), z, c))

    def step3(r):
        for k in range(2):
            @pl.when(role != k)
            def _():
                arrived(gx.at[r, x * 2 + k], R["rs2x"].at[r, k])
        for d, half in ((0, 0), (1, 1), (0, 1), (1, 0)):
            g3x(r, d, half).start()
        for o in (0, 1):
            @pl.when(role == o)
            def _():
                for d in range(1, 4):
                    arrived(gy.at[r, o * 4 + xo(d)], R["rs2y"].at[r, xo(d)])
                for cp in g3y_role(r, o):
                    cp.start()

    def forward3(r):
        for d in range(2):
            arrived(gx.at[r, xo(2 * d - 1) * 2 + d], R["rs3x"].at[r, d, d])
            g3xf(r, d).start()
        for o in range(4):
            @pl.when(role == o)
            def _():
                k, j, _d = passed[o]
                arrived(gy.at[r, half_y(k, j)], R["rs3y"].at[r, k, j])
                g3yf(r, o).start()

    def rest3(r):
        for d in range(2):
            arrived(gx.at[r, xo(2 * d - 1) * 2 + 1 - d], R["rs3x"].at[r, d, 1 - d])
        for d in range(2):
            arrived(gx.at[r, xo(2) * 2 + d], R["rs3x"].at[r, d, 2])
        for o in range(4):
            @pl.when(role == o)
            def _():
                for k in (0, 1):
                    if o == k:
                        continue
                    for j in (0, 1):
                        if (k, j) != passed[o][:2]:
                            arrived(gy.at[r, half_y(k, j)], R["rs3y"].at[r, k, j])

    part, part_in = R["part"], R["part_in"]
    ROWS = (slice(0, 256), slice(256, 512))

    def project(r, route):
        total = part[ROWS[r], :] if route else jnp.zeros((256, 256), F32)
        for k in range(2):
            for l in range(2):
                base = (k * 2 + l) * 1024
                zs = slice(l * 4, l * 4 + 4)
                if route == 0:
                    a = jnp.concatenate([gz[r, zs, k, xx].reshape(64, ZW) for xx in range(4)], axis=0)
                    total += mm(a, w[base : base + ZW, :])
                elif route == 1:
                    a = jnp.concatenate([gx[r, xx * 2 + k, zs].reshape(64, XW) for xx in range(4)], axis=0)
                    total += mm(a, w[base + XO : base + XO + XW, :])
                else:
                    a = gy[r, k * 4 : k * 4 + 4, zs].reshape(256, YW)
                    total += mm(a, w[base + YO : base + YO + YW, :])
        part[ROWS[r], :] = total

    def swap(r):
        rows = pl.ds(r * 256, 256)
        return rdma(part.at[rows], part_in.at[rows], R["ss4"].at[r], R["rs4"].at[r], partner)

    kv, kvt = R["kv"], R["kvt"]

    def keys_values(r):
        rows = ROWS[r]
        pre = part[rows, :] + part_in[rows, :]
        part_in[rows, :] = pre
        kp = pre[:, :HD]
        inv = lax.rsqrt(jnp.mean(kp * kp, axis=-1, keepdims=True) + EPS)
        keys = (kp * inv).astype(BF16)
        vals = pre[:, HD:].astype(BF16)
        kv[0, rows] = keys
        kv[1, rows] = vals
        kvt[0, :, rows] = keys.astype(F32).T.astype(BF16)
        kvt[1, :, rows] = vals.astype(F32).T.astype(BF16)

    def transpose_weights(lo, hi):
        @pl.loop(lo, hi)
        def _(n):
            rows = pl.ds(pl.multiple_of(n * 256, 256), 256)
            wt[:, rows] = w[rows, :].astype(F32).T.astype(BF16)

    step2(0)
    step2(1)
    zstep(0, 0)
    zstep(1, 0)
    for cp in wcopies:
        cp.wait()
    step3(0)
    transpose_weights(0, 8)
    zstep(0, 1)
    zstep(1, 1)
    step3(1)
    transpose_weights(8, 16)
    limits = lim[...].reshape(1, 512)
    limit = (1 - c) * limits[:, :256] + c * limits[:, 256:]
    for t in range(4):
        bias[t] = jnp.broadcast_to(jnp.where(t < limit, 0.0, -1e30), (16, 256))
    forward3(0)
    zstep(0, 2)
    zstep(1, 2)
    zstep(0, 3)
    zstep(1, 3)
    for d in range(2):
        z3_arrived(0, d, 3)
    project(0, 0)
    forward3(1)
    rest3(0)
    project(0, 1)
    project(0, 2)
    swap(0).start()
    for d in range(2):
        z3_arrived(1, d, 3)
    project(1, 0)
    swap(0).wait()
    keys_values(0)
    rest3(1)
    project(1, 1)
    project(1, 2)
    swap(1).start()
    swap(1).wait()
    keys_values(1)

    probs, dsc, at_ = R["probs"], R["dsc"], R["at"]

    @pl.loop(0, 8, unroll=4)
    def _(n):
        lanes = pl.ds(pl.multiple_of(n * 256, 256), 256)
        dotn = dot_[n]
        s = mm(kv[0], qt[n]) * (SCALE * LOG2E)
        s = (s.reshape(8, 4, 16, 256) + bias[...][None]).reshape(512, 256)
        m = jnp.max(s, axis=0, keepdims=True)
        e = jnp.exp2(s - m)
        prob = e * (1.0 / jnp.sum(e, axis=0, keepdims=True))
        pb16 = prob.astype(BF16)
        probs[:, lanes] = pb16
        at = mm(kvt[1], pb16).astype(BF16)
        at_[n] = at
        dp = mm(kv[1], dotn)
        delta = jnp.sum(at.astype(F32) * dotn.astype(F32), axis=0, keepdims=True)
        dsc[:, lanes] = (prob * (dp - delta)).astype(BF16)

    dkv, dkv_in = R["dkv"], R["dkv_in"]

    def key_grads(r):
        rows = ROWS[r]
        kp = part_in[rows, :HD]
        inv = lax.rsqrt(jnp.mean(kp * kp, axis=-1, keepdims=True) + EPS)
        dk = mm(dsc[rows, :], q[...].reshape(2048, HD)) * SCALE
        dv = mm(probs[rows, :], do[...].reshape(2048, HD))
        dkp = inv * dk - kp * (inv * inv * inv * jnp.mean(kp * dk, axis=-1, keepdims=True))
        dkv[rows, :HD] = dkp.astype(BF16)
        dkv[rows, HD:] = dv.astype(BF16)

    def swap2(r):
        rows = pl.ds(r * 256, 256)
        return rdma(dkv.at[rows], dkv_in.at[rows], R["ss4"].at[2 + r], R["rs4"].at[2 + r], partner)

    def heads_out(lo, hi):
        @pl.loop(lo, hi, unroll=2)
        def _(n):
            lanes = pl.ds(pl.multiple_of(n * HD, HD), HD)
            dqt = mm(kvt[0], dsc[:, pl.ds(pl.multiple_of(n * 256, 256), 256)]) * SCALE
            R["dq_v"][:, lanes] = dqt.T.astype(BF16)
            R["att_v"][:, lanes] = at_[n].astype(F32).T.astype(BF16)

    def back(r, route):
        for k in range(2):
            for l in range(2):
                base = (k * 2 + l) * 1024 + (0, XO, YO)[route]
                n = (ZW, XW, YW)[route]
                zs = slice(l * 4, l * 4 + 4)
                wtb = wt[:, base : base + n]
                v = (mm(dkv[ROWS[r], :], wtb) + mm(dkv_in[ROWS[r], :], wtb)).astype(BF16)
                if route == 2:
                    py[r, k * 4 : k * 4 + 4, zs] = v.reshape(4, 4, 16, YW)
                    continue
                for xx in range(4):
                    b = v[xx * 64 : (xx + 1) * 64].reshape(4, 16, n)
                    if route == 0:
                        pz[r, zs, k, xx] = b
                    else:
                        px[r, xx * 2 + k, zs] = b

    rz1 = R["rz1"]

    def rz(r, d, s):
        side = 1 - 2 * d
        at = zind(zo(side * (4 - s)))
        src = pz.at[r, at, d] if s == 0 else pz.at[r, at]
        dst = rz1.at[r, d, 0, d] if s == 0 else rz1.at[r, d, s]
        return rdma(src, dst, R["ssrz1"].at[r, d, s], R["rsrz1"].at[r, d, s], dev(x, y, zo(side), c))

    def rz_arrived(r, d, s):
        arrived(rz1.at[r, d, 0, d] if s == 0 else rz1.at[r, d, s], R["rsrz1"].at[r, d, s])

    def rzstep(r, s):
        for d in range(2):
            if s > 0:
                rz_arrived(r, d, s - 1)
                at = zind(zo((1 - 2 * d) * (4 - s)))
                if s == 1:
                    pz[r, at, d] = (pz[r, at, d].astype(F32) + rz1[r, d, 0, d].astype(F32)).astype(BF16)
                else:
                    pz[r, at] = (pz[r, at].astype(F32) + rz1[r, d, s - 1].astype(F32)).astype(BF16)
            rz(r, d, s).start()

    def rzy_to(r, k):
        return rdma(
            pz.at[r, zi, k], R["rzy"].at[r, y], R["ssrz2"].at[r, k], R["rsrz2"].at[r, y], dev(x, 2 * c + k, z, c)
        )

    def rz_sum(r):
        for d in range(2):
            rz_arrived(r, d, 3)
        pz[r, zi] = (pz[r, zi].astype(F32) + rz1[r, 0, 3].astype(F32) + rz1[r, 1, 3].astype(F32)).astype(BF16)
        for k in range(2):
            @pl.when(role != k)
            def _():
                rzy_to(r, k).start()

    def rzx_to(r, d):
        return rdma(
            R["tz"].at[r, xo(d)], R["rzx"].at[x], R["ssrz3"].at[r, d], R["rsrz3"].at[x], dev(xo(d), y, z, r)
        )

    def rzx_all(r, act):
        for d in (2, 1, 3):
            act(rzx_to(r, d))

        @pl.when(c != r)
        def _():
            act(rzx_to(r, 0))

    def rz_rows(r):
        @pl.when(home)
        def _():
            v = pz[r, zi, yp].astype(F32)
            for d in range(1, 4):
                arrived(R["rzy"].at[r, yo(d)], R["rsrz2"].at[r, yo(d)])
                v += R["rzy"][r, yo(d)].astype(F32)
            R["tz"][r] = v.astype(BF16)
            rzx_all(r, begin)

            @pl.when(c == r)
            def _():
                pltpu.make_async_copy(R["tz"].at[r, x], R["rzx"].at[x], R["rsrz3"].at[x]).start()

    def r1x_opp(r, d):
        return rdma(
            px.at[r, xo(2) * 2 + d], R["r1o"].at[r, d], R["ssr1"].at[r, 0, d], R["rsr1x"].at[r, 0, d],
            dev(xo(1 - 2 * d), y, z, c),
        )

    def r1x_free(r, d):
        return rdma(
            px.at[r, xo(1 - 2 * d) * 2 + 1 - d], R["r1n"].at[r, d, 1 - d], R["ssr1"].at[r, 0, 2 + d],
            R["rsr1x"].at[r, 1, d], dev(xo(1 - 2 * d), y, z, c),
        )

    def r1x_dep(r, d):
        return rdma(
            px.at[r, xo(1 - 2 * d) * 2 + d], R["r1n"].at[r, d, d], R["ssr1"].at[r, 0, 4 + d],
            R["rsr1x"].at[r, 2, d], dev(xo(1 - 2 * d), y, z, c),
        )

    y_opp = {2: ((1, 0, 0), (0, 0, 1)), 3: ((0, 1, 0), (1, 1, 1))}
    y_free = {0: (0, 1, 1), 1: (1, 0, 1), 2: (1, 1, 0), 3: (0, 0, 0)}
    y_dep = {0: (0, 1, 0), 1: (1, 0, 0), 2: (1, 1, 1), 3: (0, 0, 1)}

    def r1y_opp(r, o, i):
        d, k, j = y_opp[o][i]
        return rdma(
            py.at[r, half_y(k, j)], R["r1yo"].at[r], R["ssr1"].at[r, 1, i], R["rsr1y"].at[r, 0],
            dev(x, yo(1 - 2 * d), z, c),
        )

    def r1y_next(r, o, dep):
        d, k, j = (y_dep if dep else y_free)[o]
        side = 0 if o >= 2 else 1
        return rdma(
            py.at[r, half_y(k, j)], R["r1yn"].at[r, side, pl.ds(j * 2, 2)], R["ssr1"].at[r, 1, 2 + dep],
            R["rsr1y"].at[r, 1 + dep + side * 2], dev(x, yo(1 - 2 * d), z, c),
        )

    def rs1x(r):
        for d in range(2):
            r1x_opp(r, d).start()
        for d in range(2):
            r1x_free(r, d).start()

    def rs1y(r):
        for o in (2, 3):
            @pl.when(role == o)
            def _():
                for i in range(2):
                    r1y_opp(r, o, i).start()
        for o in range(4):
            @pl.when(role == o)
            def _():
                r1y_next(r, o, 0).start()

    def rs1_dep(r):
        r1o, r1yo = R["r1o"], R["r1yo"]
        for d in range(2):
            arrived(r1o.at[r, d], R["rsr1x"].at[r, 0, d])
            to = xo(1 - 2 * d) * 2 + d

            @pl.loop(0, 8, unroll=2)
            def _(i):
                px[r, to, i] = (px[r, to, i].astype(F32) + r1o[r, d, i].astype(F32)).astype(BF16)

            r1x_dep(r, d).start()
        arrived(r1yo.at[r], R["rsr1y"].at[r, 0])
        for o in range(4):
            @pl.when(role == o)
            def _():
                _d, k, j = y_dep[o]

                @pl.loop(0, 8)
                def _(i):
                    for xx in range(2):
                        at = k * 4 + j * 2 + xx
                        py[r, at, i] = (py[r, at, i].astype(F32) + r1yo[r, xx, i].astype(F32)).astype(BF16)

                r1y_next(r, o, 1).start()

    sx, sy, r2x, r2y, tx, ty = (R[n] for n in ("sx", "sy", "r2x", "r2y", "tx", "ty"))

    def r2x_to(r, k):
        return rdma(
            sx.at[r, k], r2x.at[r, y], R["ssr2"].at[r, 0, k], R["rsr2x"].at[r, y], dev(x, 2 * c + k, z, c)
        )

    def r2y_to(r, d):
        return rdma(
            sy.at[r, xo(d)], r2y.at[r, x], R["ssr2"].at[r, 1, d], R["rsr2y"].at[r, x], dev(xo(d), y, z, c)
        )

    def rs2(r):
        r1n, r1yn = R["r1n"], R["r1yn"]
        for d in range(2):
            arrived(r1n.at[r, d, 1 - d], R["rsr1x"].at[r, 1, d])
        for d in range(2):
            arrived(r1n.at[r, d, d], R["rsr1x"].at[r, 2, d])

        @pl.loop(0, 8)
        def _(b):
            for k in range(2):
                sx[r, k, b] = (
                    px[r, x * 2 + k, b].astype(F32) + r1n[r, 0, k, b].astype(F32) + r1n[r, 1, k, b].astype(F32)
                ).astype(BF16)

        for k in range(2):
            @pl.when(role != k)
            def _():
                r2x_to(r, k).start()

        @pl.when(home)
        def _():
            arrived(r1yn.at[r, 0, pl.ds(0, 2)], R["rsr1y"].at[r, 1])
            arrived(r1yn.at[r, 1, pl.ds(2, 2)], R["rsr1y"].at[r, 3])
            arrived(r1yn.at[r, 0, pl.ds(2, 2)], R["rsr1y"].at[r, 2])
            arrived(r1yn.at[r, 1, pl.ds(0, 2)], R["rsr1y"].at[r, 4])

            @pl.loop(0, 8)
            def _(b):
                for k in range(4):
                    sy[r, k, b] = (
                        py[r, yp * 4 + k, b].astype(F32) + r1yn[r, 0, k, b].astype(F32) + r1yn[r, 1, k, b].astype(F32)
                    ).astype(BF16)

            for d in (2, 1, 3):
                r2y_to(r, d).start()

    def r3_to(r, route, d):
        t, dst = ((tx, R["r3x"]), (ty, R["r3y"]))[route]
        zz = zo(d)
        return rdma(
            t.at[r, zind(zz)], dst.at[zi], R["ssr3"].at[r, route, d], R["rsr3"].at[route, zi], dev(x, y, zz, r)
        )

    def r3_all(r, route, act):
        for d in (4, 3, 5, 2, 6, 1, 7):
            act(r3_to(r, route, d))

        @pl.when(c != r)
        def _():
            act(r3_to(r, route, 0))

    def r3_own(r, route):
        t, dst = ((tx, R["r3x"]), (ty, R["r3y"]))[route]

        @pl.when(c == r)
        def _():
            pltpu.make_async_copy(t.at[r, zi], dst.at[zi], R["rsr3"].at[route, zi]).start()

    def rs3(r):
        @pl.when(home)
        def _():
            for d in range(1, 4):
                arrived(r2x.at[r, yo(d)], R["rsr2x"].at[r, yo(d)])

            @pl.loop(0, 8, unroll=2)
            def _(b):
                v = sx[r, yp, b].astype(F32)
                for d in range(1, 4):
                    v += r2x[r, yo(d), b].astype(F32)
                tx[r, b] = v.astype(BF16)

            r3_all(r, 0, begin)
            r3_own(r, 0)
            for d in range(1, 4):
                arrived(r2y.at[r, xo(d)], R["rsr2y"].at[r, xo(d)])

            @pl.loop(0, 8, unroll=2)
            def _(b):
                v = sy[r, x, b].astype(F32)
                for d in range(1, 4):
                    v += r2y[r, xo(d), b].astype(F32)
                ty[r, b] = v.astype(BF16)

            r3_all(r, 1, begin)
            r3_own(r, 1)

    def finish(route):
        src, n, o = ((R["r3x"], XW, XO), (R["r3y"], YW, YO))[route]
        for b in range(8):
            arrived(src.at[b], R["rsr3"].at[route, b])
        total = src[0].astype(F32)
        for b in range(1, 8):
            total += src[b].astype(F32)
        R["gv_v"][:, o : o + n] = total

    def finish_z():
        for b in range(4):
            arrived(R["rzx"].at[b], R["rsrz3"].at[b])
        total = R["rzx"][0].astype(F32)
        for b in range(1, 4):
            total += R["rzx"][b].astype(F32)
        R["gv_v"][:, :ZW] = total

    outs = [
        pltpu.make_async_copy(R["att_v"], att_o.at[0], R["osem"].at[0]),
        pltpu.make_async_copy(R["dq_v"], dq_o.at[0], R["osem"].at[1]),
        pltpu.make_async_copy(R["gv_v"], gv_o, R["osem"].at[2]),
    ]

    key_grads(0)
    swap2(0).start()
    key_grads(1)
    swap2(1).start()
    swap2(0).wait()
    for r in range(2):
        if r == 1:
            swap2(1).wait()
        back(r, 0)
        for d in range(2):
            rz(r, d, 0).start()
        back(r, 1)
        rs1x(r)
        back(r, 2)
        rs1y(r)
    heads_out(0, 4)
    rs1_dep(0)
    rzstep(0, 1)
    rzstep(1, 1)
    heads_out(4, 8)
    for cp in outs[:2]:
        cp.start()
    rs1_dep(1)
    rzstep(0, 2)
    rzstep(1, 2)
    rs2(0)
    rzstep(0, 3)
    rzstep(1, 3)
    rs2(1)
    rs3(0)
    rz_sum(0)
    rz_sum(1)
    rz_rows(0)
    rz_rows(1)
    rs3(1)
    finish_z()
    finish(0)
    finish(1)
    outs[2].start()

    z1_all(sent)
    for route in range(2):
        g1_all(route, sent)
    for r in range(2):
        @pl.when(home)
        def _():
            for d in range(1, 4):
                sent(z2(r, d))
                sent(g2x(r, d))
                sent(g2y(r, d))
                sent(r2y_to(r, d))
            for route in range(2):
                r3_all(r, route, sent)
            rzx_all(r, sent)

        for d in range(2):
            for s in range(4):
                sent(z3(r, d, s))
                sent(rz(r, d, s))
            for half in range(2):
                sent(g3x(r, d, half))
            sent(g3xf(r, d))
            sent(r1x_opp(r, d))
            sent(r1x_free(r, d))
            sent(r1x_dep(r, d))
        for o in range(4):
            @pl.when(role == o)
            def _():
                if o < 2:
                    for cp in g3y_role(r, o):
                        sent(cp)
                else:
                    for i in range(2):
                        sent(r1y_opp(r, o, i))
                sent(g3yf(r, o))
                sent(r1y_next(r, o, 0))
                sent(r1y_next(r, o, 1))
        for k in range(2):
            @pl.when(role != k)
            def _():
                sent(r2x_to(r, k))
                sent(rzy_to(r, k))
    for cp in outs:
        cp.wait()


def copy_out(a, b, d, ao, bo, do, av, bv, dv, sems):
    moves = ((a, av, ao), (b, bv, bo), (d, dv, do))
    loads = [pltpu.make_async_copy(s, v, sems.at[0, i]) for i, (s, v, _) in enumerate(moves)]
    stores = [pltpu.make_async_copy(v, t, sems.at[1, i]) for i, (_, v, t) in enumerate(moves)]
    for cp in loads:
        cp.start()
    for load, store in zip(loads, stores):
        load.wait()
        store.start()
    for cp in stores:
        cp.wait()


def on_device(queries, grad_attended, vision, key_weight, value_weight, tile_limit):
    vmem = pl.BlockSpec(memory_space=pltpu.VMEM)
    hbm = pl.BlockSpec(memory_space=pl.ANY)
    shapes = (
        jax.ShapeDtypeStruct(queries.shape, BF16),
        jax.ShapeDtypeStruct(queries.shape, BF16),
        jax.ShapeDtypeStruct(vision.shape, F32),
    )
    outs = pl.pallas_call(
        kernel,
        out_shape=shapes,
        in_specs=[hbm, hbm, hbm, hbm, hbm, vmem],
        out_specs=(hbm, hbm, hbm),
        scratch_shapes=list(scratch().values()),
        compiler_params=pltpu.CompilerParams(
            collective_id=0, has_side_effects=True, vmem_limit_bytes=60 * 2**20
        ),
        cost_estimate=pl.CostEstimate(flops=6_000_000_000, bytes_accessed=6_000_000, transcendentals=1_000_000),
    )(vision, key_weight, value_weight, queries, grad_attended, tile_limit)
    return pl.pallas_call(
        copy_out,
        out_shape=shapes,
        in_specs=[hbm, hbm, hbm],
        out_specs=(hbm, hbm, hbm),
        scratch_shapes=[pltpu.VMEM(s.shape, s.dtype) for s in shapes] + [pltpu.SemaphoreType.DMA((2, 3))],
    )(*outs)


def solution(mesh):
    return jax.shard_map(
        on_device,
        mesh=mesh,
        in_specs=(
            P("segment", None, "tensor"),
            P("segment", None, "tensor"),
            P("segment", "tensor"),
            P("segment", None, "tensor"),
            P("segment", None, "tensor"),
            P(),
        ),
        out_specs=(
            P("segment", None, "tensor"),
            P("segment", None, "tensor"),
            P("segment", "tensor"),
        ),
        check_vma=False,
    )
```

time: 321 us -> 89.3 us (0.28); the launches traced: 317 us -> 89.1 us
  waiting for transfers between devices: 215 us -> 0 us
  Pallas kernels: 0 us -> 88.5 us
  matrix products: 32 us -> 0 us
  blocking collectives: 26.7 us -> 0 us
  between operations: 13.9 us -> 0.64 us
  other arithmetic: 12.6 us -> 0 us
  local copies, waits for them, and re-layouts: 8.76 us -> 0 us
  starting transfers between devices: 8.02 us -> 0 us
    reduce_scatter x2 -> x0, waiting for transfers between devices: 155 us -> none  [the longest x1 121 us: on_device(): lax.psum_scatter((term + jnp.dot(grad_vals, value_matrix.T, preferred_ele...]
    pallas_call x0 -> x2, Pallas kernels: none -> 88.5 us  [the longest x1 86.4 us: on_device(): pl.pallas_call(kernel, out_shape=shapes, in_specs=[hbm, hbm, hbm, hbm, hb...]
    all_gather x1 -> x0, waiting for transfers between devices: 59.6 us -> none  [on_device(): lax.all_gather(widened, 'segment', axis=0, tiled=True)]
    dot_general x8 -> x0, matrix products: 32 us -> none  [the longest x1 11.6 us: on_device(): jnp.dot(grad_vals, value_matrix.T, preferred_element_type=jnp.float32)]
    all_gather x1 -> x0, blocking collectives: 26.7 us -> none  [on_device(): widened = lax.all_gather(vision, 'tensor', axis=1, tiled=True)]
    squeeze x1 -> x0, other arithmetic: 8.28 us -> none  [on_device(): key_matrix = full_weights[0]]
    ppermute x1 -> x0, starting transfers between devices: 7.89 us -> none  [from_partner(): return lax.ppermute(value, axis, pairs)]
    unnamed x22 -> x0, local copies, waits for them, and re-layouts: 4.97 us -> none
  transfers between devices with their start and end apart: 4 -> 0, of which waited for: 4 -> 0; matrix products, arithmetic and copies ran while one was open for 6% -> 0% of each run, Pallas kernels for 0% -> 0%
where the time goes in v3:
time: 89.3 us; the launch traced here: 89.1 us
  Pallas kernels  88.5 us (99%)
    pallas_call x1, Pallas kernels, on_device(): pl.pallas_call(kernel, out_shape=shapes, in_specs=[hbm, hbm, hbm, hbm, hb...  86.4 us
    pallas_call x1, Pallas kernels, on_device(): pl.pallas_call(copy_out, out_shape=shapes, in_specs=[hbm, hbm, hbm], out_...  2.07 us

profile of v3, /device:TPU:1, one launch (start us, length us, event | category | flops | bytes accessed | tf_op | source)
XLA Modules:
  0.0 89.1 jit_solution(15403093248483003065)
XLA Ops:
  0.6 86.4 %shard_map.85 = (bf16[1,256,1024]{2,1,0:T(8,128)(2,1)}, bf16[1,256,1024]{2,1,0:T(8,128)(2,1)}, f32[16,1024]{1,0:T(8,128)}) custom-call(bf16[16,1024]{1,0:T(8,128)(2,1)} %vis.1, bf16[1,4096,128]{2,1,0:T(8,128)(2,1)} %wk.1, bf16[1,4096,128]{2,1,0:T(8,128)(2,1)} %wv.1, bf16[1,256,1024]{2,1,0:T(8,128)(2,1)} %q_in.1, bf16[1,256,1024]{2,1,0:T(8,128)(2,1)} %do_in.1, ...), custom_call_target="tpu_custom_call" | custom-call | flops 6000000000 | bytes 6000000 | tf_op jit(solution)/shard_map/pallas_call | solution.py:821
  87.0 2.1 %shard_map.86 = (bf16[1,256,1024]{2,1,0:T(8,128)(2,1)}, bf16[1,256,1024]{2,1,0:T(8,128)(2,1)}, f32[16,1024]{1,0:T(8,128)}) custom-call(bf16[1,256,1024]{2,1,0:T(8,128)(2,1)} %get-tuple-element.6.a, bf16[1,256,1024]{2,1,0:T(8,128)(2,1)} %get-tuple-element.7.b, f32[16,1024]{1,0:T(8,128)} %get-tuple-element.8.d), custom_call_target="tpu_custom_call" | custom-call | tf_op jit(solution)/shard_map/pallas_call | solution.py:832

commit v4 on v3

--- a/solution.py
+++ b/solution.py
@@ -40,18 +40,14 @@
         "r2x": v((2, 4, 8, 16, XW), BF16), "r2y": v((2, 4, 8, 16, YW), BF16),
         "tx": v((2, 8, 16, XW), BF16), "ty": v((2, 8, 16, YW), BF16),
         "r3x": v((8, 16, XW), BF16), "r3y": v((8, 16, YW), BF16),
-        "lsem": dma((8,)), "osem": dma((3,)),
-        "ss1": dma((2, 8)), "rs1": dma((2, 2, 8)),
-        "ss2": dma((2, 2, 4)), "rs2x": dma((2, 2)), "rs2y": dma((2, 4)),
-        "ss3": dma((2, 2, 2, 3)), "rs3x": dma((2, 2, 3)), "rs3y": dma((2, 2, 2)),
-        "ss4": dma((4,)), "rs4": dma((4,)),
-        "ssr1": dma((2, 2, 6)), "rsr1x": dma((2, 3, 2)), "rsr1y": dma((2, 5)),
-        "ssr2": dma((2, 2, 4)), "rsr2x": dma((2, 4)), "rsr2y": dma((2, 4)),
-        "ssr3": dma((2, 2, 8)), "rsr3": dma((2, 8)),
-        "ssz1": dma((4,)), "rsz1": dma((2, 4)), "ssz2": dma((2, 4)), "rsz2": dma((2, 2)),
-        "ssz3": dma((2, 2, 4)), "rsz3": dma((2, 2, 4)),
-        "ssrz1": dma((2, 2, 4)), "rsrz1": dma((2, 2, 4)),
-        "ssrz2": dma((2, 2)), "rsrz2": dma((2, 4)), "ssrz3": dma((2, 4)), "rsrz3": dma((4,)),
+        "lsem": dma((4,)), "osem": dma((3,)), "ss4": dma((4,)), "rs4": dma((4,)),
+        "ssz1": dma((1,)), "ss1": dma((2,)), "ssz2": dma((2,)), "ss2": dma((2, 2)), "ss3": dma((2, 2)),
+        "ssz3": dma((2,)), "ssrz1": dma((2,)), "ssr1": dma((2, 2)), "ssr2": dma((2, 2)), "ssr3": dma((2, 2)),
+        "ssrz2": dma((2,)), "ssrz3": dma((2,)),
+        "rsz1": dma((2,)), "rs1": dma((2, 2)), "rsz2": dma((2,)), "rs2x": dma((2,)), "rs2y": dma((2,)),
+        "rs3x": dma((2, 3)), "rs3y": dma((2, 2)), "rsz3": dma((2, 7)),
+        "rsrz1": dma((2, 7)), "rsr1x": dma((2, 3)), "rsr1y": dma((2, 2)), "rsr2x": dma((2,)), "rsr2y": dma((2,)),
+        "rsr3": dma((2,)), "rsrz2": dma((2,)), "rsrz3": dma((1,)),
     }
     return s
 
@@ -105,8 +101,8 @@
     def begin(cp):
         cp.start()
 
-    def sent(cp):
-        cp.wait_send()
+    def sent(ref, ss):
+        rdma(ref, ref, ss, R["rs4"].at[0], partner).wait_send()
 
     lsem = R["lsem"]
     wcopies = [
@@ -131,7 +127,7 @@
     pl.semaphore_wait(barrier, len(greet))
 
     def z1(d):
-        return rdma(vis.at[:, pl.ds(0, ZW)], gz.at[c, zi, yp, x], R["ssz1"].at[d], R["rsz1"].at[c, x], dev(xo(d), y, z, h))
+        return rdma(vis.at[:, pl.ds(0, ZW)], gz.at[c, zi, yp, x], R["ssz1"].at[0], R["rsz1"].at[c], dev(xo(d), y, z, h))
 
     def z1_all(act):
         for d in (2, 1, 3):
@@ -146,7 +142,7 @@
             (vis.at[:, pl.ds(XO, XW)], gx.at[c, x * 2 + yp, zi]),
             (vis.at[:, pl.ds(YO, YW)], gy.at[c, yp * 4 + x, zi]),
         )[route]
-        return rdma(src, dst, R["ss1"].at[route, d], R["rs1"].at[c, route, zi], dev(x, y, zo(d), h))
+        return rdma(src, dst, R["ss1"].at[route], R["rs1"].at[c, route], dev(x, y, zo(d), h))
 
     def g1_all(route, act):
         for d in (4, 3, 5, 2, 6, 1, 7):
@@ -162,9 +158,9 @@
 
     @pl.when(home)
     def _():
-        pltpu.make_async_copy(vis.at[:, pl.ds(0, ZW)], gz.at[c, zi, yp, x], R["rsz1"].at[c, x]).start()
-        pltpu.make_async_copy(vis.at[:, pl.ds(XO, XW)], gx.at[c, x * 2 + yp, zi], R["rs1"].at[c, 0, zi]).start()
-        pltpu.make_async_copy(vis.at[:, pl.ds(YO, YW)], gy.at[c, yp * 4 + x, zi], R["rs1"].at[c, 1, zi]).start()
+        pltpu.make_async_copy(vis.at[:, pl.ds(0, ZW)], gz.at[c, zi, yp, x], R["rsz1"].at[c]).start()
+        pltpu.make_async_copy(vis.at[:, pl.ds(XO, XW)], gx.at[c, x * 2 + yp, zi], R["rs1"].at[c, 0]).start()
+        pltpu.make_async_copy(vis.at[:, pl.ds(YO, YW)], gy.at[c, yp * 4 + x, zi], R["rs1"].at[c, 1]).start()
 
     for cp in loads:
         cp.wait()
@@ -182,52 +178,64 @@
 
     def z2(r, d):
         blk = gz.at[r, zi, yp]
-        return rdma(blk, blk, R["ssz2"].at[r, d], R["rsz2"].at[r, yp], dev(x, yo(d), z, c))
+        return rdma(blk, blk, R["ssz2"].at[r], R["rsz2"].at[r], dev(x, yo(d), z, c))
 
     @pl.when(home)
     def _():
         for r in range(2):
-            for xx in range(4):
-                arrived(gz.at[r, zi, yp, xx], R["rsz1"].at[r, xx])
+            arrived(gz.at[r, zi, yp], R["rsz1"].at[r])
             for d in (2, 1, 3):
                 z2(r, d).start()
 
     def g2x(r, d):
         blk = gx.at[r, x * 2 + yp]
-        return rdma(blk, blk, R["ss2"].at[r, 0, d], R["rs2x"].at[r, yp], dev(x, yo(d), z, c))
+        return rdma(blk, blk, R["ss2"].at[r, 0], R["rs2x"].at[r], dev(x, yo(d), z, c))
 
     def g2y(r, d):
         blk = gy.at[r, yp * 4 + x]
-        return rdma(blk, blk, R["ss2"].at[r, 1, d], R["rs2y"].at[r, x], dev(xo(d), y, z, c))
-
-    def step2(r):
+        return rdma(blk, blk, R["ss2"].at[r, 1], R["rs2y"].at[r], dev(xo(d), y, z, c))
+
+    def step2x(r):
         @pl.when(home)
         def _():
-            for zz in range(8):
-                arrived(gx.at[r, x * 2 + yp, zz], R["rs1"].at[r, 0, zz])
+            arrived(gx.at[r, x * 2 + yp], R["rs1"].at[r, 0])
             for d in (2, 1, 3):
                 g2x(r, d).start()
-            for zz in range(8):
-                arrived(gy.at[r, yp * 4 + x, zz], R["rs1"].at[r, 1, zz])
+
+    def step2y(r):
+        @pl.when(home)
+        def _():
+            arrived(gy.at[r, yp * 4 + x], R["rs1"].at[r, 1])
             for d in (2, 1, 3):
                 g2y(r, d).start()
+
+    def by_home(few, many):
+        @pl.when(home)
+        def _():
+            few()
+
+        @pl.when(c == 1 - h)
+        def _():
+            many()
 
     def z3(r, d, s):
         side = 1 - 2 * d
         at = zind(zo(-side * s))
         blk = gz.at[r, at] if s < 3 else gz.at[r, at, d]
-        return rdma(blk, blk, R["ssz3"].at[r, d, s], R["rsz3"].at[r, d, s], dev(x, y, zo(side), c))
+        return rdma(blk, blk, R["ssz3"].at[r], R["rsz3"].at[r, s * 2 + d if s < 3 else 6], dev(x, y, zo(side), c))
 
     def z3_arrived(r, d, s):
-        at = zind(zo(-(1 - 2 * d) * (s + 1)))
-        arrived(gz.at[r, at] if s < 3 else gz.at[r, at, d], R["rsz3"].at[r, d, s])
+        arrived(gz.at[r, zind(zo(-(1 - 2 * d) * (s + 1)))], R["rsz3"].at[r, s * 2 + d])
+
+    def z3_last(r):
+        arrived(gz.at[r, zind(zo(4))], R["rsz3"].at[r, 6])
 
     def zstep(r, s):
         if s == 0:
-            for k in range(2):
-                @pl.when(role != k)
-                def _():
-                    arrived(gz.at[r, zi, k], R["rsz2"].at[r, k])
+            by_home(
+                lambda: arrived(gz.at[r, zi, 1 - yp], R["rsz2"].at[r]),
+                lambda: arrived(gz.at[r, zi], R["rsz2"].at[r]),
+            )
         for d in range(2):
             if s > 0:
                 z3_arrived(r, d, s - 1)
@@ -235,76 +243,72 @@
 
     def g3x(r, d, half):
         blk = gx.at[r, x * 2 + half]
-        return rdma(blk, blk, R["ss3"].at[r, 0, d, half], R["rs3x"].at[r, d, half], dev(xo(1 - 2 * d), y, z, c))
+        return rdma(blk, blk, R["ss3"].at[r, 0], R["rs3x"].at[r, d if half == d else 2], dev(xo(1 - 2 * d), y, z, c))
 
     def g3xf(r, d):
         blk = gx.at[r, xo(2 * d - 1) * 2 + d]
-        return rdma(blk, blk, R["ss3"].at[r, 0, d, 2], R["rs3x"].at[r, d, 2], dev(xo(1 - 2 * d), y, z, c))
+        return rdma(blk, blk, R["ss3"].at[r, 0], R["rs3x"].at[r, 2], dev(xo(1 - 2 * d), y, z, c))
 
     def half_y(k, j):
         return pl.ds(k * 4 + j * 2, 2)
 
-    def g3y(r, k, j, d):
+    passed = ((1, 0, 1), (0, 0, 0), (1, 1, 0), (0, 1, 1))
+
+    def g3y(r, o, k, j, d):
         blk = gy.at[r, half_y(k, j)]
-        return rdma(blk, blk, R["ss3"].at[r, 1, d, j], R["rs3y"].at[r, k, j], dev(x, yo(1 - 2 * d), z, c))
+        first = passed[(o + 1 - 2 * d) % 4][:2] == (k, j)
+        return rdma(blk, blk, R["ss3"].at[r, 1], R["rs3y"].at[r, 0 if first else 1], dev(x, yo(1 - 2 * d), z, c))
 
     def g3y_role(r, o):
         order = ((0, 0, 0), (0, 1, 1), (0, 1, 0), (0, 0, 1)) if o == 0 else ((1, 0, 1), (1, 1, 0), (1, 1, 1), (1, 0, 0))
-        return [g3y(r, k, j, d) for k, j, d in order]
-
-    passed = ((1, 0, 1), (0, 0, 0), (1, 1, 0), (0, 1, 1))
+        return [g3y(r, o, k, j, d) for k, j, d in order]
 
     def g3yf(r, o):
         k, j, d = passed[o]
-        blk = gy.at[r, half_y(k, j)]
-        return rdma(blk, blk, R["ss3"].at[r, 1, d, 2], R["rs3y"].at[r, k, j], dev(x, yo(1 - 2 * d), z, c))
-
-    def step3(r):
-        for k in range(2):
-            @pl.when(role != k)
-            def _():
-                arrived(gx.at[r, x * 2 + k], R["rs2x"].at[r, k])
+        return g3y(r, o, k, j, d)
+
+    def step3x(r):
+        by_home(
+            lambda: arrived(gx.at[r, x * 2 + 1 - yp], R["rs2x"].at[r]),
+            lambda: arrived(gx.at[r, pl.ds(x * 2, 2)], R["rs2x"].at[r]),
+        )
         for d, half in ((0, 0), (1, 1), (0, 1), (1, 0)):
             g3x(r, d, half).start()
+
+    def step3y(r):
         for o in (0, 1):
             @pl.when(role == o)
             def _():
-                for d in range(1, 4):
-                    arrived(gy.at[r, o * 4 + xo(d)], R["rs2y"].at[r, xo(d)])
+                arrived(gy.at[r, pl.ds(o * 4, 3)], R["rs2y"].at[r])
                 for cp in g3y_role(r, o):
                     cp.start()
 
-    def forward3(r):
+    def forward3x(r):
         for d in range(2):
-            arrived(gx.at[r, xo(2 * d - 1) * 2 + d], R["rs3x"].at[r, d, d])
+            arrived(gx.at[r, xo(2 * d - 1) * 2 + d], R["rs3x"].at[r, d])
             g3xf(r, d).start()
+
+    def forward3y(r):
         for o in range(4):
             @pl.when(role == o)
             def _():
-                k, j, _d = passed[o]
-                arrived(gy.at[r, half_y(k, j)], R["rs3y"].at[r, k, j])
+                arrived(gy.at[r, half_y(*passed[o][:2])], R["rs3y"].at[r, 0])
                 g3yf(r, o).start()
 
-    def rest3(r):
-        for d in range(2):
-            arrived(gx.at[r, xo(2 * d - 1) * 2 + 1 - d], R["rs3x"].at[r, d, 1 - d])
-        for d in range(2):
-            arrived(gx.at[r, xo(2) * 2 + d], R["rs3x"].at[r, d, 2])
-        for o in range(4):
-            @pl.when(role == o)
-            def _():
-                for k in (0, 1):
-                    if o == k:
-                        continue
-                    for j in (0, 1):
-                        if (k, j) != passed[o][:2]:
-                            arrived(gy.at[r, half_y(k, j)], R["rs3y"].at[r, k, j])
+    def rest3x(r):
+        arrived(gx.at[r, pl.ds(0, 4)], R["rs3x"].at[r, 2])
+
+    def rest3y(r):
+        by_home(
+            lambda: arrived(gy.at[r, pl.ds(0, 2)], R["rs3y"].at[r, 1]),
+            lambda: arrived(gy.at[r, pl.ds(0, 6)], R["rs3y"].at[r, 1]),
+        )
 
     part, part_in = R["part"], R["part_in"]
     ROWS = (slice(0, 256), slice(256, 512))
 
     def project(r, route):
-        total = part[ROWS[r], :] if route else jnp.zeros((256, 256), F32)
+        total = part[ROWS[r], :] if route != (1, 0)[r] else jnp.zeros((256, 256), F32)
         for k in range(2):
             for l in range(2):
                 base = (k * 2 + l) * 1024
@@ -345,42 +349,48 @@
             rows = pl.ds(pl.multiple_of(n * 256, 256), 256)
             wt[:, rows] = w[rows, :].astype(F32).T.astype(BF16)
 
-    step2(0)
-    step2(1)
+    step2x(0)
+    step2x(1)
+    step2y(0)
+    step2y(1)
     zstep(0, 0)
     zstep(1, 0)
     for cp in wcopies:
         cp.wait()
-    step3(0)
+    step3x(0)
+    step3y(0)
+    step3x(1)
+    step3y(1)
     transpose_weights(0, 8)
     zstep(0, 1)
     zstep(1, 1)
-    step3(1)
     transpose_weights(8, 16)
     limits = lim[...].reshape(1, 512)
     limit = (1 - c) * limits[:, :256] + c * limits[:, 256:]
     for t in range(4):
         bias[t] = jnp.broadcast_to(jnp.where(t < limit, 0.0, -1e30), (16, 256))
-    forward3(0)
+    forward3x(0)
+    forward3y(0)
     zstep(0, 2)
     zstep(1, 2)
+    forward3x(1)
+    forward3y(1)
     zstep(0, 3)
     zstep(1, 3)
-    for d in range(2):
-        z3_arrived(0, d, 3)
+    rest3x(0)
+    project(0, 1)
+    rest3y(0)
+    project(0, 2)
+    z3_last(0)
     project(0, 0)
-    forward3(1)
-    rest3(0)
-    project(0, 1)
-    project(0, 2)
     swap(0).start()
-    for d in range(2):
-        z3_arrived(1, d, 3)
+    z3_last(1)
     project(1, 0)
     swap(0).wait()
     keys_values(0)
-    rest3(1)
+    rest3x(1)
     project(1, 1)
+    rest3y(1)
     project(1, 2)
     swap(1).start()
     swap(1).wait()
@@ -454,10 +464,10 @@
         at = zind(zo(side * (4 - s)))
         src = pz.at[r, at, d] if s == 0 else pz.at[r, at]
         dst = rz1.at[r, d, 0, d] if s == 0 else rz1.at[r, d, s]
-        return rdma(src, dst, R["ssrz1"].at[r, d, s], R["rsrz1"].at[r, d, s], dev(x, y, zo(side), c))
+        return rdma(src, dst, R["ssrz1"].at[r], R["rsrz1"].at[r, s * 2 + d if s < 3 else 6], dev(x, y, zo(side), c))
 
     def rz_arrived(r, d, s):
-        arrived(rz1.at[r, d, 0, d] if s == 0 else rz1.at[r, d, s], R["rsrz1"].at[r, d, s])
+        arrived(rz1.at[r, d, 0, d] if s == 0 else rz1.at[r, d, s], R["rsrz1"].at[r, s * 2 + d])
 
     def rzstep(r, s):
         for d in range(2):
@@ -472,12 +482,11 @@
 
     def rzy_to(r, k):
         return rdma(
-            pz.at[r, zi, k], R["rzy"].at[r, y], R["ssrz2"].at[r, k], R["rsrz2"].at[r, y], dev(x, 2 * c + k, z, c)
+            pz.at[r, zi, k], R["rzy"].at[r, y], R["ssrz2"].at[r], R["rsrz2"].at[r], dev(x, 2 * c + k, z, c)
         )
 
     def rz_sum(r):
-        for d in range(2):
-            rz_arrived(r, d, 3)
+        arrived(rz1.at[r, 0, pl.ds(2, 2)], R["rsrz1"].at[r, 6])
         pz[r, zi] = (pz[r, zi].astype(F32) + rz1[r, 0, 3].astype(F32) + rz1[r, 1, 3].astype(F32)).astype(BF16)
         for k in range(2):
             @pl.when(role != k)
@@ -486,7 +495,7 @@
 
     def rzx_to(r, d):
         return rdma(
-            R["tz"].at[r, xo(d)], R["rzx"].at[x], R["ssrz3"].at[r, d], R["rsrz3"].at[x], dev(xo(d), y, z, r)
+            R["tz"].at[r, xo(d)], R["rzx"].at[x], R["ssrz3"].at[r], R["rsrz3"].at[0], dev(xo(d), y, z, r)
         )
 
     def rzx_all(r, act):
@@ -500,33 +509,33 @@
     def rz_rows(r):
         @pl.when(home)
         def _():
+            arrived(R["rzy"].at[r, pl.ds(0, 3)], R["rsrz2"].at[r])
             v = pz[r, zi, yp].astype(F32)
             for d in range(1, 4):
-                arrived(R["rzy"].at[r, yo(d)], R["rsrz2"].at[r, yo(d)])
                 v += R["rzy"][r, yo(d)].astype(F32)
             R["tz"][r] = v.astype(BF16)
             rzx_all(r, begin)
 
             @pl.when(c == r)
             def _():
-                pltpu.make_async_copy(R["tz"].at[r, x], R["rzx"].at[x], R["rsrz3"].at[x]).start()
+                pltpu.make_async_copy(R["tz"].at[r, x], R["rzx"].at[x], R["rsrz3"].at[0]).start()
 
     def r1x_opp(r, d):
         return rdma(
-            px.at[r, xo(2) * 2 + d], R["r1o"].at[r, d], R["ssr1"].at[r, 0, d], R["rsr1x"].at[r, 0, d],
+            px.at[r, xo(2) * 2 + d], R["r1o"].at[r, d], R["ssr1"].at[r, 0], R["rsr1x"].at[r, d],
             dev(xo(1 - 2 * d), y, z, c),
         )
 
     def r1x_free(r, d):
         return rdma(
-            px.at[r, xo(1 - 2 * d) * 2 + 1 - d], R["r1n"].at[r, d, 1 - d], R["ssr1"].at[r, 0, 2 + d],
-            R["rsr1x"].at[r, 1, d], dev(xo(1 - 2 * d), y, z, c),
+            px.at[r, xo(1 - 2 * d) * 2 + 1 - d], R["r1n"].at[r, d, 1 - d], R["ssr1"].at[r, 0],
+            R["rsr1x"].at[r, 2], dev(xo(1 - 2 * d), y, z, c),
         )
 
     def r1x_dep(r, d):
         return rdma(
-            px.at[r, xo(1 - 2 * d) * 2 + d], R["r1n"].at[r, d, d], R["ssr1"].at[r, 0, 4 + d],
-            R["rsr1x"].at[r, 2, d], dev(xo(1 - 2 * d), y, z, c),
+            px.at[r, xo(1 - 2 * d) * 2 + d], R["r1n"].at[r, d, d], R["ssr1"].at[r, 0],
+            R["rsr1x"].at[r, 2], dev(xo(1 - 2 * d), y, z, c),
         )
 
     y_opp = {2: ((1, 0, 0), (0, 0, 1)), 3: ((0, 1, 0), (1, 1, 1))}
@@ -536,7 +545,7 @@
     def r1y_opp(r, o, i):
         d, k, j = y_opp[o][i]
         return rdma(
-            py.at[r, half_y(k, j)], R["r1yo"].at[r], R["ssr1"].at[r, 1, i], R["rsr1y"].at[r, 0],
+            py.at[r, half_y(k, j)], R["r1yo"].at[r], R["ssr1"].at[r, 1], R["rsr1y"].at[r, 0],
             dev(x, yo(1 - 2 * d), z, c),
         )
 
@@ -544,31 +553,36 @@
         d, k, j = (y_dep if dep else y_free)[o]
         side = 0 if o >= 2 else 1
         return rdma(
-            py.at[r, half_y(k, j)], R["r1yn"].at[r, side, pl.ds(j * 2, 2)], R["ssr1"].at[r, 1, 2 + dep],
-            R["rsr1y"].at[r, 1 + dep + side * 2], dev(x, yo(1 - 2 * d), z, c),
-        )
-
-    def rs1x(r):
+            py.at[r, half_y(k, j)], R["r1yn"].at[r, side, pl.ds(j * 2, 2)], R["ssr1"].at[r, 1],
+            R["rsr1y"].at[r, 1], dev(x, yo(1 - 2 * d), z, c),
+        )
+
+    def opp_x(r):
         for d in range(2):
             r1x_opp(r, d).start()
+
+    def free_x(r):
         for d in range(2):
             r1x_free(r, d).start()
 
-    def rs1y(r):
+    def opp_y(r):
         for o in (2, 3):
             @pl.when(role == o)
             def _():
                 for i in range(2):
                     r1y_opp(r, o, i).start()
+
+    def free_y(r):
         for o in range(4):
             @pl.when(role == o)
             def _():
                 r1y_next(r, o, 0).start()
 
-    def rs1_dep(r):
-        r1o, r1yo = R["r1o"], R["r1yo"]
+    r1o, r1yo, r1n, r1yn = (R[n] for n in ("r1o", "r1yo", "r1n", "r1yn"))
+
+    def dep_x(r):
         for d in range(2):
-            arrived(r1o.at[r, d], R["rsr1x"].at[r, 0, d])
+            arrived(r1o.at[r, d], R["rsr1x"].at[r, d])
             to = xo(1 - 2 * d) * 2 + d
 
             @pl.loop(0, 8, unroll=2)
@@ -576,6 +590,7 @@
                 px[r, to, i] = (px[r, to, i].astype(F32) + r1o[r, d, i].astype(F32)).astype(BF16)
 
             r1x_dep(r, d).start()
+    def dep_y(r):
         arrived(r1yo.at[r], R["rsr1y"].at[r, 0])
         for o in range(4):
             @pl.when(role == o)
@@ -594,20 +609,16 @@
 
     def r2x_to(r, k):
         return rdma(
-            sx.at[r, k], r2x.at[r, y], R["ssr2"].at[r, 0, k], R["rsr2x"].at[r, y], dev(x, 2 * c + k, z, c)
+            sx.at[r, k], r2x.at[r, y], R["ssr2"].at[r, 0], R["rsr2x"].at[r], dev(x, 2 * c + k, z, c)
         )
 
     def r2y_to(r, d):
         return rdma(
-            sy.at[r, xo(d)], r2y.at[r, x], R["ssr2"].at[r, 1, d], R["rsr2y"].at[r, x], dev(xo(d), y, z, c)
-        )
-
-    def rs2(r):
-        r1n, r1yn = R["r1n"], R["r1yn"]
-        for d in range(2):
-            arrived(r1n.at[r, d, 1 - d], R["rsr1x"].at[r, 1, d])
-        for d in range(2):
-            arrived(r1n.at[r, d, d], R["rsr1x"].at[r, 2, d])
+            sy.at[r, xo(d)], r2y.at[r, x], R["ssr2"].at[r, 1], R["rsr2y"].at[r], dev(xo(d), y, z, c)
+        )
+
+    def rs2x(r):
+        arrived(r1n.at[r], R["rsr1x"].at[r, 2])
 
         @pl.loop(0, 8)
         def _(b):
@@ -621,12 +632,10 @@
             def _():
                 r2x_to(r, k).start()
 
+    def rs2y(r):
         @pl.when(home)
         def _():
-            arrived(r1yn.at[r, 0, pl.ds(0, 2)], R["rsr1y"].at[r, 1])
-            arrived(r1yn.at[r, 1, pl.ds(2, 2)], R["rsr1y"].at[r, 3])
-            arrived(r1yn.at[r, 0, pl.ds(2, 2)], R["rsr1y"].at[r, 2])
-            arrived(r1yn.at[r, 1, pl.ds(0, 2)], R["rsr1y"].at[r, 4])
+            arrived(r1yn.at[r], R["rsr1y"].at[r, 1])
 
             @pl.loop(0, 8)
             def _(b):
@@ -642,7 +651,7 @@
         t, dst = ((tx, R["r3x"]), (ty, R["r3y"]))[route]
         zz = zo(d)
         return rdma(
-            t.at[r, zind(zz)], dst.at[zi], R["ssr3"].at[r, route, d], R["rsr3"].at[route, zi], dev(x, y, zz, r)
+            t.at[r, zind(zz)], dst.at[zi], R["ssr3"].at[r, route], R["rsr3"].at[route], dev(x, y, zz, r)
         )
 
     def r3_all(r, route, act):
@@ -658,13 +667,12 @@
 
         @pl.when(c == r)
         def _():
-            pltpu.make_async_copy(t.at[r, zi], dst.at[zi], R["rsr3"].at[route, zi]).start()
-
-    def rs3(r):
+            pltpu.make_async_copy(t.at[r, zi], dst.at[zi], R["rsr3"].at[route]).start()
+
+    def rs3x(r):
         @pl.when(home)
         def _():
-            for d in range(1, 4):
-                arrived(r2x.at[r, yo(d)], R["rsr2x"].at[r, yo(d)])
+            arrived(r2x.at[r, pl.ds(0, 3)], R["rsr2x"].at[r])
 
             @pl.loop(0, 8, unroll=2)
             def _(b):
@@ -675,8 +683,11 @@
 
             r3_all(r, 0, begin)
             r3_own(r, 0)
-            for d in range(1, 4):
-                arrived(r2y.at[r, xo(d)], R["rsr2y"].at[r, xo(d)])
+
+    def rs3y(r):
+        @pl.when(home)
+        def _():
+            arrived(r2y.at[r, pl.ds(0, 3)], R["rsr2y"].at[r])
 
             @pl.loop(0, 8, unroll=2)
             def _(b):
@@ -690,16 +701,14 @@
 
     def finish(route):
         src, n, o = ((R["r3x"], XW, XO), (R["r3y"], YW, YO))[route]
-        for b in range(8):
-            arrived(src.at[b], R["rsr3"].at[route, b])
+        arrived(src, R["rsr3"].at[route])
         total = src[0].astype(F32)
         for b in range(1, 8):
             total += src[b].astype(F32)
         R["gv_v"][:, o : o + n] = total
 
     def finish_z():
-        for b in range(4):
-            arrived(R["rzx"].at[b], R["rsrz3"].at[b])
+        arrived(R["rzx"], R["rsrz3"].at[0])
         total = R["rzx"][0].astype(F32)
         for b in range(1, 4):
             total += R["rzx"][b].astype(F32)
@@ -716,83 +725,108 @@
     key_grads(1)
     swap2(1).start()
     swap2(0).wait()
-    for r in range(2):
-        if r == 1:
-            swap2(1).wait()
-        back(r, 0)
-        for d in range(2):
-            rz(r, d, 0).start()
-        back(r, 1)
-        rs1x(r)
-        back(r, 2)
-        rs1y(r)
+    back(0, 0)
+    for d in range(2):
+        rz(0, d, 0).start()
+    back(0, 1)
+    opp_x(0)
+    free_x(0)
+    back(0, 2)
+    opp_y(0)
+    free_y(0)
+    swap2(1).wait()
+    back(1, 0)
+    for d in range(2):
+        rz(1, d, 0).start()
+    back(1, 1)
+    opp_x(1)
+    free_x(1)
+    back(1, 2)
+    opp_y(1)
+    free_y(1)
     heads_out(0, 4)
-    rs1_dep(0)
+    dep_x(0)
+    dep_y(0)
     rzstep(0, 1)
     rzstep(1, 1)
     heads_out(4, 8)
     for cp in outs[:2]:
         cp.start()
-    rs1_dep(1)
+    dep_x(1)
+    dep_y(1)
     rzstep(0, 2)
     rzstep(1, 2)
-    rs2(0)
+    rs2x(0)
+    rs2y(0)
     rzstep(0, 3)
     rzstep(1, 3)
-    rs2(1)
-    rs3(0)
+    rs2x(1)
+    rs2y(1)
+    rs3x(0)
+    rs3y(0)
     rz_sum(0)
     rz_sum(1)
     rz_rows(0)
     rz_rows(1)
-    rs3(1)
+    rs3x(1)
+    rs3y(1)
     finish_z()
     finish(0)
     finish(1)
     outs[2].start()
 
-    z1_all(sent)
-    for route in range(2):
-        g1_all(route, sent)
+    by_home(
+        lambda: sent(gz.at[0, 0, 0, pl.ds(0, 3)], R["ssz1"].at[0]),
+        lambda: sent(gz.at[0, 0, 0], R["ssz1"].at[0]),
+    )
+    for i, ref in enumerate((gx, gy)):
+        by_home(
+            lambda: sent(ref.at[0, 0, pl.ds(0, 7)], R["ss1"].at[i]),
+            lambda: sent(ref.at[0, 0], R["ss1"].at[i]),
+        )
     for r in range(2):
+        sent(gz.at[r, pl.ds(0, 7)], R["ssz3"].at[r])
+        sent(pz.at[r, pl.ds(0, 7)], R["ssrz1"].at[r])
+        sent(gx.at[r, pl.ds(0, 6)], R["ss3"].at[r, 0])
+        sent(px.at[r, pl.ds(0, 6)], R["ssr1"].at[r, 0])
+
         @pl.when(home)
         def _():
-            for d in range(1, 4):
-                sent(z2(r, d))
-                sent(g2x(r, d))
-                sent(g2y(r, d))
-                sent(r2y_to(r, d))
-            for route in range(2):
-                r3_all(r, route, sent)
-            rzx_all(r, sent)
-
-        for d in range(2):
-            for s in range(4):
-                sent(z3(r, d, s))
-                sent(rz(r, d, s))
-            for half in range(2):
-                sent(g3x(r, d, half))
-            sent(g3xf(r, d))
-            sent(r1x_opp(r, d))
-            sent(r1x_free(r, d))
-            sent(r1x_dep(r, d))
-        for o in range(4):
-            @pl.when(role == o)
-            def _():
-                if o < 2:
-                    for cp in g3y_role(r, o):
-                        sent(cp)
-                else:
-                    for i in range(2):
-                        sent(r1y_opp(r, o, i))
-                sent(g3yf(r, o))
-                sent(r1y_next(r, o, 0))
-                sent(r1y_next(r, o, 1))
-        for k in range(2):
-            @pl.when(role != k)
-            def _():
-                sent(r2x_to(r, k))
-                sent(rzy_to(r, k))
+            sent(R["rzy"].at[r, pl.ds(0, 3)], R["ssz2"].at[r])
+            sent(gx.at[r, pl.ds(0, 3)], R["ss2"].at[r, 0])
+            sent(gy.at[r, pl.ds(0, 3)], R["ss2"].at[r, 1])
+            sent(sy.at[r, pl.ds(0, 3)], R["ssr2"].at[r, 1])
+            sent(gy.at[:, pl.ds(0, 5)], R["ss3"].at[r, 1])
+
+            @pl.when(c == r)
+            def _():
+                sent(tx.at[r, pl.ds(0, 7)], R["ssr3"].at[r, 0])
+                sent(ty.at[r, pl.ds(0, 7)], R["ssr3"].at[r, 1])
+                sent(R["tz"].at[r, pl.ds(0, 3)], R["ssrz3"].at[r])
+
+            @pl.when(c != r)
+            def _():
+                sent(tx.at[r], R["ssr3"].at[r, 0])
+                sent(ty.at[r], R["ssr3"].at[r, 1])
+                sent(R["tz"].at[r], R["ssrz3"].at[r])
+
+        by_home(
+            lambda: sent(py.at[r, pl.ds(0, 4)], R["ssr1"].at[r, 1]),
+            lambda: sent(py.at[r], R["ssr1"].at[r, 1]),
+        )
+        by_home(
+            lambda: sent(sx.at[r, 0], R["ssr2"].at[r, 0]),
+            lambda: sent(sx.at[r], R["ssr2"].at[r, 0]),
+        )
+        by_home(
+            lambda: sent(pz.at[r, 0, 0], R["ssrz2"].at[r]),
+            lambda: sent(pz.at[r, 0], R["ssrz2"].at[r]),
+        )
+
+        @pl.when(c == 1 - h)
+        def _():
+            sent(gy.at[r, pl.ds(0, 2)], R["ss3"].at[r, 1])
+
     for cp in outs:
         cp.wait()
 

time: 89.3 us -> 83.5 us (0.935)
  Pallas kernels: 88.5 us -> 82.7 us
    pallas_call x1, Pallas kernels: 86.4 us -> 80.6 us  [on_device(): pl.pallas_call(kernel, out_shape=shapes, in_specs=[hbm, hbm, hbm, hbm, hb...]
where the time goes in v4:
time: 83.5 us; the launch traced here: 83.4 us
  Pallas kernels  82.7 us (99%)
    pallas_call x1, Pallas kernels, on_device(): pl.pallas_call(kernel, out_shape=shapes, in_specs=[hbm, hbm, hbm, hbm, hb...  80.6 us
    pallas_call x1, Pallas kernels, on_device(): pl.pallas_call(copy_out, out_shape=shapes, in_specs=[hbm, hbm, hbm], out_...  2.07 us

profile of v4, /device:TPU:1, one launch (start us, length us, event | category | flops | bytes accessed | tf_op | source)
XLA Modules:
  0.0 83.4 jit_solution(3849683618322073981)
XLA Ops:
  0.6 80.6 %shard_map.85 = (bf16[1,256,1024]{2,1,0:T(8,128)(2,1)}, bf16[1,256,1024]{2,1,0:T(8,128)(2,1)}, f32[16,1024]{1,0:T(8,128)}) custom-call(bf16[16,1024]{1,0:T(8,128)(2,1)} %vis.1, bf16[1,4096,128]{2,1,0:T(8,128)(2,1)} %wk.1, bf16[1,4096,128]{2,1,0:T(8,128)(2,1)} %wv.1, bf16[1,256,1024]{2,1,0:T(8,128)(2,1)} %q_in.1, bf16[1,256,1024]{2,1,0:T(8,128)(2,1)} %do_in.1, ...), custom_call_target="tpu_custom_call" | custom-call | flops 6000000000 | bytes 6000000 | tf_op jit(solution)/shard_map/pallas_call | solution.py:855
  81.3 2.1 %shard_map.86 = (bf16[1,256,1024]{2,1,0:T(8,128)(2,1)}, bf16[1,256,1024]{2,1,0:T(8,128)(2,1)}, f32[16,1024]{1,0:T(8,128)}) custom-call(bf16[1,256,1024]{2,1,0:T(8,128)(2,1)} %get-tuple-element.6.a, bf16[1,256,1024]{2,1,0:T(8,128)(2,1)} %get-tuple-element.7.b, f32[16,1024]{1,0:T(8,128)} %get-tuple-element.8.d), custom_call_target="tpu_custom_call" | custom-call | tf_op jit(solution)/shard_map/pallas_call | solution.py:866

commit v5 on v4

--- a/solution.py
+++ b/solution.py
@@ -20,6 +20,7 @@
 def scratch():
     v, dma = pltpu.VMEM, pltpu.SemaphoreType.DMA
     s = {
+        "vis": v((16, 1024), BF16),
         "q": v((8, 256, 128), BF16), "do": v((8, 256, 128), BF16),
         "w": v((4096, 256), BF16), "wt": v((256, 4096), BF16),
         "qt": v((8, 128, 256), BF16), "dot": v((8, 128, 256), BF16),
@@ -40,7 +41,7 @@
         "r2x": v((2, 4, 8, 16, XW), BF16), "r2y": v((2, 4, 8, 16, YW), BF16),
         "tx": v((2, 8, 16, XW), BF16), "ty": v((2, 8, 16, YW), BF16),
         "r3x": v((8, 16, XW), BF16), "r3y": v((8, 16, YW), BF16),
-        "lsem": dma((4,)), "osem": dma((3,)), "ss4": dma((4,)), "rs4": dma((4,)),
+        "lsem": dma((5,)), "osem": dma((3,)), "ss4": dma((4,)), "rs4": dma((4,)),
         "ssz1": dma((1,)), "ss1": dma((2,)), "ssz2": dma((2,)), "ss2": dma((2, 2)), "ss3": dma((2, 2)),
         "ssz3": dma((2,)), "ssrz1": dma((2,)), "ssr1": dma((2, 2)), "ssr2": dma((2, 2)), "ssr3": dma((2, 2)),
         "ssrz2": dma((2,)), "ssrz3": dma((2,)),
@@ -59,9 +60,9 @@
     return jnp.dot(a, b, preferred_element_type=F32)
 
 
-def kernel(vis, wk, wv, q_in, do_in, lim, att_o, dq_o, gv_o, *rest):
+def kernel(vis_in, wk, wv, q_in, do_in, lim, att_o, dq_o, gv_o, *rest):
     R = dict(zip(NAMES, rest, strict=True))
-    q, do, w, wt = R["q"], R["do"], R["w"], R["wt"]
+    vis, q, do, w, wt = R["vis"], R["q"], R["do"], R["w"], R["wt"]
     gx, gy, gz, px, py, pz = (R[n] for n in ("gx", "gy", "gz", "px", "py", "pz"))
 
     seg, ten = lax.axis_index("segment"), lax.axis_index("tensor")
@@ -114,6 +115,8 @@
     greet = [dev(x, y, zo(d), cc) for d in range(1, 8) for cc in (0, 1)]
     greet += [dev(xo(d), y, z, cc) for d in range(1, 4) for cc in (0, 1)]
     greet += [dev(x, yo(d), z, c) for d in range(1, 4)] + [partner]
+    shard = pltpu.make_async_copy(vis_in, vis, lsem.at[4])
+    shard.start()
     for other in greet:
         pl.semaphore_signal(barrier, inc=1, device_id=other, device_id_type=MESH)
     for cp in wcopies:
@@ -124,6 +127,7 @@
     ]
     for cp in loads:
         cp.start()
+    shard.wait()
     pl.semaphore_wait(barrier, len(greet))
 
     def z1(d):
@@ -398,7 +402,7 @@
 
     probs, dsc, at_ = R["probs"], R["dsc"], R["at"]
 
-    @pl.loop(0, 8, unroll=4)
+    @pl.loop(0, 8, unroll=8)
     def _(n):
         lanes = pl.ds(pl.multiple_of(n * 256, 256), 256)
         dotn = dot_[n]
@@ -439,6 +443,11 @@
             R["dq_v"][:, lanes] = dqt.T.astype(BF16)
             R["att_v"][:, lanes] = at_[n].astype(F32).T.astype(BF16)
 
+    def both(r):
+        swap2(r).wait()
+        rows = ROWS[r]
+        dkv[rows, :] = (dkv[rows, :].astype(F32) + dkv_in[rows, :].astype(F32)).astype(BF16)
+
     def back(r, route):
         for k in range(2):
             for l in range(2):
@@ -446,7 +455,7 @@
                 n = (ZW, XW, YW)[route]
                 zs = slice(l * 4, l * 4 + 4)
                 wtb = wt[:, base : base + n]
-                v = (mm(dkv[ROWS[r], :], wtb) + mm(dkv_in[ROWS[r], :], wtb)).astype(BF16)
+                v = mm(dkv[ROWS[r], :], wtb).astype(BF16)
                 if route == 2:
                     py[r, k * 4 : k * 4 + 4, zs] = v.reshape(4, 4, 16, YW)
                     continue
@@ -724,38 +733,38 @@
     swap2(0).start()
     key_grads(1)
     swap2(1).start()
-    swap2(0).wait()
+    both(0)
+    back(0, 1)
+    opp_x(0)
+    free_x(0)
     back(0, 0)
     for d in range(2):
         rz(0, d, 0).start()
-    back(0, 1)
-    opp_x(0)
-    free_x(0)
     back(0, 2)
     opp_y(0)
     free_y(0)
-    swap2(1).wait()
+    both(1)
+    back(1, 1)
+    opp_x(1)
+    back(1, 2)
+    opp_y(1)
     back(1, 0)
     for d in range(2):
         rz(1, d, 0).start()
-    back(1, 1)
-    opp_x(1)
+    dep_x(0)
     free_x(1)
-    back(1, 2)
-    opp_y(1)
+    dep_y(0)
     free_y(1)
-    heads_out(0, 4)
-    dep_x(0)
-    dep_y(0)
     rzstep(0, 1)
     rzstep(1, 1)
-    heads_out(4, 8)
-    for cp in outs[:2]:
-        cp.start()
+    heads_out(0, 4)
     dep_x(1)
     dep_y(1)
     rzstep(0, 2)
     rzstep(1, 2)
+    heads_out(4, 8)
+    for cp in outs[:2]:
+        cp.start()
     rs2x(0)
     rs2y(0)
     rzstep(0, 3)

time: 83.5 us -> 81.8 us (0.980)
  Pallas kernels: 82.7 us -> 81 us
    pallas_call x1, Pallas kernels: 80.6 us -> 78.9 us  [on_device(): pl.pallas_call(kernel, out_shape=shapes, in_specs=[hbm, hbm, hbm, hbm, hb...]
where the time goes in v5:
time: 81.8 us; the launch traced here: 81.7 us
  Pallas kernels  81 us (99%)
    pallas_call x1, Pallas kernels, on_device(): pl.pallas_call(kernel, out_shape=shapes, in_specs=[hbm, hbm, hbm, hbm, hb...  78.9 us
    pallas_call x1, Pallas kernels, on_device(): pl.pallas_call(copy_out, out_shape=shapes, in_specs=[hbm, hbm, hbm], out_...  2.07 us

profile of v5, /device:TPU:1, one launch (start us, length us, event | category | flops | bytes accessed | tf_op | source)
XLA Modules:
  0.0 81.7 jit_solution(1314526605221619599)
XLA Ops:
  0.6 78.9 %shard_map.85 = (bf16[1,256,1024]{2,1,0:T(8,128)(2,1)}, bf16[1,256,1024]{2,1,0:T(8,128)(2,1)}, f32[16,1024]{1,0:T(8,128)}) custom-call(bf16[16,1024]{1,0:T(8,128)(2,1)} %vis_in.1, bf16[1,4096,128]{2,1,0:T(8,128)(2,1)} %wk.1, bf16[1,4096,128]{2,1,0:T(8,128)(2,1)} %wv.1, bf16[1,256,1024]{2,1,0:T(8,128)(2,1)} %q_in.1, bf16[1,256,1024]{2,1,0:T(8,128)(2,1)} %do_in.1, ...), custom_call_target="tpu_custom_call" | custom-call | flops 6000000000 | bytes 6000000 | tf_op jit(solution)/shard_map/pallas_call | solution.py:864
  79.6 2.1 %shard_map.86 = (bf16[1,256,1024]{2,1,0:T(8,128)(2,1)}, bf16[1,256,1024]{2,1,0:T(8,128)(2,1)}, f32[16,1024]{1,0:T(8,128)}) custom-call(bf16[1,256,1024]{2,1,0:T(8,128)(2,1)} %get-tuple-element.6.a, bf16[1,256,1024]{2,1,0:T(8,128)(2,1)} %get-tuple-element.7.b, f32[16,1024]{1,0:T(8,128)} %get-tuple-element.8.d), custom_call_target="tpu_custom_call" | custom-call | tf_op jit(solution)/shard_map/pallas_call | solution.py:875

commit v6 on v5

--- a/solution.py
+++ b/solution.py
@@ -775,10 +775,10 @@
     rs3y(0)
     rz_sum(0)
     rz_sum(1)
+    rs3x(1)
+    rs3y(1)
     rz_rows(0)
     rz_rows(1)
-    rs3x(1)
-    rs3y(1)
     finish_z()
     finish(0)
     finish(1)

time: 81.8 us -> 79.5 us (0.972)
  Pallas kernels: 81 us -> 78.7 us
    pallas_call x1, Pallas kernels: 78.9 us -> 76.7 us  [on_device(): pl.pallas_call(kernel, out_shape=shapes, in_specs=[hbm, hbm, hbm, hbm, hb...]
where the time goes in v6:
time: 79.5 us; the launch traced here: 79.4 us
  Pallas kernels  78.7 us (99%)
    pallas_call x1, Pallas kernels, on_device(): pl.pallas_call(kernel, out_shape=shapes, in_specs=[hbm, hbm, hbm, hbm, hb...  76.7 us
    pallas_call x1, Pallas kernels, on_device(): pl.pallas_call(copy_out, out_shape=shapes, in_specs=[hbm, hbm, hbm], out_...  2.07 us

profile of v6, /device:TPU:1, one launch (start us, length us, event | category | flops | bytes accessed | tf_op | source)
XLA Modules:
  0.0 79.4 jit_solution(14305784433567185475)
XLA Ops:
  0.6 76.7 %shard_map.85 = (bf16[1,256,1024]{2,1,0:T(8,128)(2,1)}, bf16[1,256,1024]{2,1,0:T(8,128)(2,1)}, f32[16,1024]{1,0:T(8,128)}) custom-call(bf16[16,1024]{1,0:T(8,128)(2,1)} %vis_in.1, bf16[1,4096,128]{2,1,0:T(8,128)(2,1)} %wk.1, bf16[1,4096,128]{2,1,0:T(8,128)(2,1)} %wv.1, bf16[1,256,1024]{2,1,0:T(8,128)(2,1)} %q_in.1, bf16[1,256,1024]{2,1,0:T(8,128)(2,1)} %do_in.1, ...), custom_call_target="tpu_custom_call" | custom-call | flops 6000000000 | bytes 6000000 | tf_op jit(solution)/shard_map/pallas_call | solution.py:864
  77.3 2.1 %shard_map.86 = (bf16[1,256,1024]{2,1,0:T(8,128)(2,1)}, bf16[1,256,1024]{2,1,0:T(8,128)(2,1)}, f32[16,1024]{1,0:T(8,128)}) custom-call(bf16[1,256,1024]{2,1,0:T(8,128)(2,1)} %get-tuple-element.6.a, bf16[1,256,1024]{2,1,0:T(8,128)(2,1)} %get-tuple-element.7.b, f32[16,1024]{1,0:T(8,128)} %get-tuple-element.8.d), custom_call_target="tpu_custom_call" | custom-call | tf_op jit(solution)/shard_map/pallas_call | solution.py:875

commit v7 on v6

--- a/solution.py
+++ b/solution.py
@@ -737,12 +737,12 @@
     back(0, 1)
     opp_x(0)
     free_x(0)
+    back(0, 2)
+    opp_y(0)
+    free_y(0)
     back(0, 0)
     for d in range(2):
         rz(0, d, 0).start()
-    back(0, 2)
-    opp_y(0)
-    free_y(0)
     both(1)
     back(1, 1)
     opp_x(1)

time: 79.5 us -> 79.6 us (level)
  no operation moved by 1% of the time
where the time goes in v7:
time: 79.6 us; the launch traced here: 79.5 us
  Pallas kernels  78.8 us (99%)
    pallas_call x1, Pallas kernels, on_device(): pl.pallas_call(kernel, out_shape=shapes, in_specs=[hbm, hbm, hbm, hbm, hb...  76.7 us
    pallas_call x1, Pallas kernels, on_device(): pl.pallas_call(copy_out, out_shape=shapes, in_specs=[hbm, hbm, hbm], out_...  2.07 us

profile of v7, /device:TPU:1, one launch (start us, length us, event | category | flops | bytes accessed | tf_op | source)
XLA Modules:
  0.0 79.5 jit_solution(2689426361794945661)
XLA Ops:
  0.6 76.7 %shard_map.85 = (bf16[1,256,1024]{2,1,0:T(8,128)(2,1)}, bf16[1,256,1024]{2,1,0:T(8,128)(2,1)}, f32[16,1024]{1,0:T(8,128)}) custom-call(bf16[16,1024]{1,0:T(8,128)(2,1)} %vis_in.1, bf16[1,4096,128]{2,1,0:T(8,128)(2,1)} %wk.1, bf16[1,4096,128]{2,1,0:T(8,128)(2,1)} %wv.1, bf16[1,256,1024]{2,1,0:T(8,128)(2,1)} %q_in.1, bf16[1,256,1024]{2,1,0:T(8,128)(2,1)} %do_in.1, ...), custom_call_target="tpu_custom_call" | custom-call | flops 6000000000 | bytes 6000000 | tf_op jit(solution)/shard_map/pallas_call | solution.py:864
  77.4 2.1 %shard_map.86 = (bf16[1,256,1024]{2,1,0:T(8,128)(2,1)}, bf16[1,256,1024]{2,1,0:T(8,128)(2,1)}, f32[16,1024]{1,0:T(8,128)}) custom-call(bf16[1,256,1024]{2,1,0:T(8,128)(2,1)} %get-tuple-element.6.a, bf16[1,256,1024]{2,1,0:T(8,128)(2,1)} %get-tuple-element.7.b, f32[16,1024]{1,0:T(8,128)} %get-tuple-element.8.d), custom_call_target="tpu_custom_call" | custom-call | tf_op jit(solution)/shard_map/pallas_call | solution.py:875
